TPU v7x, 32 devices: a whole 2x2x4 slice. The times are simulated.
32 devices in a mesh: rows: 16 (over z, y, x), cols: 2 (over core).
Axes of the slice: x: 2, y: 2, z: 4, core: 2. Of those that a mesh axis runs over, the one named last changes fastest.
Arguments:
- block_vector: float32 [131072, 128], P('rows'), may hold values from -6 to 6
- op_tiles: float32 [1024, 8, 128, 128], P('rows', 'cols')
- tile_cols: int32 [1024, 8], P('rows', 'cols'), may hold values from 0 to 1023, as said below
- live_counts: int32 [1024], P('rows'), may hold values from 1 to 8
Outputs:
- basis_block: float32 [131072, 128], P(('rows', 'cols'))
- r_factor: float32 [128, 128], replicated
Inputs may be any that keep to these rules, and one draw needn't show every extreme that they name: `tile_cols`: slot 0 of row block i names i itself. Every entry names a row block of the same index of rows as i, or of the index just before or after it.
All inputs are finite; a program needn't handle non-finite values.
Results may differ from a plain program's by a relative error of at most 0.0003.
Values sent between devices are 32-bit elements; how exact they have to be, the bound alone decides.
A program may use at most 128 MiB of HBM per device.

v0:
```python
import jax
import jax.numpy as jnp
from jax import lax
from jax.sharding import PartitionSpec as P


def with_halo(cells, sides, width):
    for axis, dim in sides:
        count = lax.axis_size(axis)
        ends = count - 1
        head = lax.slice_in_dim(cells, 0, width, axis=dim)
        tail = lax.slice_in_dim(cells, cells.shape[dim] - width, cells.shape[dim], axis=dim)
        cells = jnp.concatenate(
            [
                lax.ppermute(tail, axis, [(i, (i + 1) % count) for i in range(ends)]),
                cells,
                lax.ppermute(head, axis, [((i + 1) % count, i) for i in range(ends)]),
            ],
            axis=dim,
        )
    return cells


def on_device(block_vector, op_tiles, tile_cols, live_counts):
    block_count, slot_count, tile_size, _ = op_tiles.shape
    vec_width = block_vector.shape[1]
    row_devices = lax.axis_size("rows")
    rows_here = block_count * tile_size
    extended = with_halo(block_vector, (("rows", 0),), rows_here)
    vec_blocks = extended.reshape(3 * block_count, tile_size, vec_width)
    first_block = lax.axis_index("rows") * block_count - block_count
    local_idx = tile_cols - first_block
    slot_ids = lax.axis_index("cols") * slot_count + jnp.arange(slot_count, dtype=jnp.int32)
    live_mask = (slot_ids[None, :] < live_counts[:, None]).astype(jnp.float32)
    picked = vec_blocks[local_idx] * live_mask[:, :, None, None]
    partial_value = jnp.einsum("jsab,jsbc->jac", op_tiles, picked, precision=lax.Precision.HIGHEST)
    partial_value = partial_value.reshape(rows_here, vec_width)
    part_rows = lax.psum_scatter(partial_value, "cols", scatter_dimension=0, tiled=True)
    local_gram = jnp.einsum("ra,rb->ab", part_rows, part_rows, precision=lax.Precision.HIGHEST)
    gram_matrix = lax.psum(local_gram, ("rows", "cols"))
    chol_lower = jnp.linalg.cholesky(gram_matrix)
    solved = jax.scipy.linalg.solve_triangular(chol_lower, part_rows.T, lower=True)
    root_nodes = jnp.sqrt(jnp.float32(rows_here * row_devices))
    return (solved.T * root_nodes, chol_lower.T / root_nodes)


def solution(mesh):
    in_specs = (P("rows", None), P("rows", "cols", None, None), P("rows", "cols"), P("rows"))
    out_specs = (P(("rows", "cols"), None), P())
    return jax.shard_map(
        on_device, mesh=mesh, in_specs=in_specs, out_specs=out_specs, check_vma=False
    )
```

profile of v0, /device:TPU:2, one launch (start us, length us, event | category | flops | bytes accessed | tf_op | source)
XLA Modules:
  0.0 419.7 jit_solution(2785916556613844385)
XLA Ops:
  7.2 0.0 reduce-scatter.2.cloned.1.call-start
  7.2 3.4 collective-permute-start
  10.6 4.4 %collective-permute-start.1 = (f32[8192,128]{1,0:T(8,128)}, f32[8192,128]{1,0:T(8,128)}, u32[]{:S(2)}, u32[]{:S(2)}) collective-permute-start(f32[8192,128]{1,0:T(8,128)} %param.4), channel_id=1, source_target_pairs={{2,0},{4,2},{6,4},{8,6},{10,8},{12,10},{14,12},{16,14},{18,16},{20... | collective-permute-start | bytes 12582920 | tf_op jit(solution)/shard_map/ppermute | solution.py:17
  15.0 0.7 compare_select_fusion
  15.7 0.1 copy.13
  15.8 0.1 reshape.57
  15.9 0.7 compare_convert_fusion
  16.7 0.1 copy.14
  16.8 174.8 %collective-permute-done = f32[8192,128]{1,0:T(8,128)} collective-permute-done((f32[8192,128]{1,0:T(8,128)}, f32[8192,128]{1,0:T(8,128)}, u32[]{:S(2)}, u32[]{:S(2)}) %collective-permute-start) | collective-permute-done | bytes 4194336 | tf_op jit(solution)/shard_map/ppermute | solution.py:15
  191.6 1.0 collective-permute-done.1
  192.6 12.5 %pad_maximum_fusion = f32[24576,128]{1,0:T(8,128)} fusion(f32[8192,128]{1,0:T(8,128)} %collective-permute-done.1, f32[8192,128]{1,0:T(8,128)} %param.4, f32[8192,128]{1,0:T(8,128)} %collective-permute-done), kind=kLoop, calls=%fused_computation.3 | loop fusion | flops 6291456 | bytes 25165824 | tf_op jit(solution)/shard_map/concatenate | solution.py:13
  205.1 16.5 %gather_fusion = f32[256,128,128]{2,1,0:T(8,128)} fusion(f32[192,128,128]{2,1,0:T(8,128)} %bitcast.23, s32[1024]{0:T(1024)S(1)} %pad_clamp_fusion), kind=kCustom, calls=%fused_computation | custom fusion | bytes 33555456 | tf_op jit(solution)/shard_map/gather | solution.py:35
  221.6 24.3 %fusion = f32[64,128,128,1]{1,2,3,0:T(8,128)} fusion(f32[64,4,128,128]{3,2,1,0:T(8,128)} %param.5, f32[64,4,128,128]{3,2,1,0:T(8,128)} %bitcast.24, f32[64,4]{1,0:T(8,128)S(1)} %copy.14), kind=kOutput, calls=%fused_computation.1 | convolution fusion | flops 6446645248 | bytes 37749760 | tf_op jit(solution)/shard_map/jsab,jsbc->jac/dot_general | solution.py:36
  245.9 0.0 reduce-scatter.2.cloned.1.call-update
  245.9 0.2 all-reduce.2.cloned.1.call-start
  246.1 12.6 %reduce-scatter.2.cloned.1.call-done = f32[4096,128]{1,0:T(8,128)} async-done(((f32[8192,128]{1,0:T(8,128)}), f32[4096,128]{1,0:T(8,128)}) %reduce-scatter.2.cloned.1.call-update) | async-done | bytes 2097168 | tf_op jit(solution)/shard_map/reduce_scatter | solution.py:38
  258.8 0.0 copy-start
  258.8 6.5 %fusion.5 = f32[128,128]{0,1:T(8,128)} fusion(f32[4096,128]{1,0:T(8,128)} %reduce-scatter.2.cloned.1.call-done), kind=kOutput, calls=%fused_computation.20 | convolution fusion | flops 805306368 | bytes 2162688 | tf_op jit(solution)/shard_map/ra,rb->ab/dot_general | solution.py:39
  265.2 0.0 all-reduce.2.cloned.1.call-update
  265.3 119.0 %all-reduce.2.cloned.1.call-done = f32[128,128]{0,1:T(8,128)} async-done(((f32[128,128]{0,1:T(8,128)}), f32[128,128]{0,1:T(8,128)}) %all-reduce.2.cloned.1.call-update) | async-done | bytes 65552 | tf_op jit(solution)/shard_map/psum | solution.py:40
  384.3 0.9 copy.16
  385.2 0.9 fusion.4
  386.1 11.7 %cholesky.16 = f32[128,128]{1,0:T(8,128)S(1)} custom-call(f32[128,128]{1,0:T(8,128)S(1)} %fusion.4), custom_call_target="Cholesky" | custom-call | tf_op jit(solution)/shard_map/jit(cholesky)/cholesky | solution.py:41
  397.9 0.6 compare_reduce_fusion
  398.5 0.7 multiply_bitcast_fusion
  399.2 9.8 %custom-call.7 = f32[1,128,128]{1,2,0:T(8,128)S(1)} custom-call(f32[1,128,128]{2,1,0:T(8,128)S(1)} %get-tuple-element.9), custom_call_target="InvertDiagBlocksLowerTriangular" | custom-call | tf_op jit(solution)/shard_map/jit(_solve_triangular)/triangular_solve | solution.py:42
  409.0 0.7 copy.17
  409.7 0.0 copy-done
  409.7 3.1 convolution_multiply_fusion
  (3 shorter events, 0.0 us)
Async XLA Ops:
  7.2 251.6 %reduce-scatter.2.cloned.1.call-start = ((), (), s32[]{:S(2)}) async-start(), calls=%async_computation.1 | async-start | bytes 6291456 | tf_op jit(solution)/shard_map/reduce_scatter | solution.py:38
  7.2 184.4 %collective-permute-start = (f32[8192,128]{1,0:T(8,128)}, f32[8192,128]{1,0:T(8,128)}, u32[]{:S(2)}, u32[]{:S(2)}) collective-permute-start(f32[8192,128]{1,0:T(8,128)} %param.4), channel_id=1, source_target_pairs={{0,2},{2,4},{4,6},{6,8},{8,10},{10,12},{12,14},{14,16},{16,18},{18... | collective-permute-start | bytes 12582920 | tf_op jit(solution)/shard_map/ppermute | solution.py:15
  10.6 182.0 %collective-permute-start.1 = (f32[8192,128]{1,0:T(8,128)}, f32[8192,128]{1,0:T(8,128)}, u32[]{:S(2)}, u32[]{:S(2)}) collective-permute-start(f32[8192,128]{1,0:T(8,128)} %param.4), channel_id=1, source_target_pairs={{2,0},{4,2},{6,4},{8,6},{10,8},{12,10},{14,12},{16,14},{18,16},{20... | collective-permute-start | bytes 12582920 | tf_op jit(solution)/shard_map/ppermute | solution.py:17
  245.9 138.4 %all-reduce.2.cloned.1.call-start = ((), (), s32[]{:S(2)}) async-start(), calls=%async_computation.2 | async-start | bytes 131072 | tf_op jit(solution)/shard_map/psum | solution.py:40
  258.8 150.9 %copy-start = (f32[4096,128]{1,0:T(8,128)S(1)}, f32[4096,128]{1,0:T(8,128)}, u32[]{:S(2)}) copy-start(f32[4096,128]{1,0:T(8,128)} %reduce-scatter.2.cloned.1.call-done) | copy-start | bytes 6291460
Sparse Core Ops, SparseCore 0:
  246.0 12.7 reduce-scatter.1
  265.9 118.4 all-reduce.1
where the time goes:
time: 423 us; the launch traced here: 420 us
  waiting for transfers between devices  308 us (73%)
  other arithmetic  37.7 us (9%)
  matrix products  33.9 us (8%)
  local copies, waits for them, and re-layouts  18.4 us (4%)
  between operations  14.1 us (3%)
  starting transfers between devices  8.06 us (2%)
    ppermute x1, waiting for transfers between devices, with_halo(): lax.ppermute(tail, axis, [(i, (i + 1) % count) for i in range(ends)])  175 us
    psum x1, waiting for transfers between devices, on_device(): gram_matrix = lax.psum(local_gram, ('rows', 'cols'))  119 us
    dot_general x1, matrix products, on_device(): jnp.einsum('jsab,jsbc->jac', op_tiles, picked, precision=lax.Precision.HI...  24.3 us
    gather x1, local copies, waits for them, and re-layouts, on_device(): picked = vec_blocks[local_idx] * live_mask[:, :, None, None]  16.5 us
    reduce_scatter x1, waiting for transfers between devices, on_device(): lax.psum_scatter(partial_value, 'cols', scatter_dimension=0, tiled=True)  12.6 us
    concatenate x1, other arithmetic, with_halo(): jnp.concatenate([lax.ppermute(tail, axis, [(i, (i + 1) % count) for i in...  12.5 us
    another operation x3, other arithmetic, on_device(): chol_lower = jnp.linalg.cholesky(gram_matrix)  12.4 us
    another operation x1, other arithmetic, on_device(): jax.scipy.linalg.solve_triangular(chol_lower, part_rows.T, lower=True)  9.81 us
  transfers between devices with their start and end apart: 4, of which 4 were waited for; matrix products, arithmetic and copies ran while one was open for 0% of the time, Pallas kernels for 0%

commit v1 on v0

v1 whole, which is shorter than its diff:
```python
import functools
import math

import jax
import jax.numpy as jnp
from jax import lax
from jax.experimental import pallas as pl
from jax.experimental.pallas import tpu as pltpu
from jax.sharding import PartitionSpec as P

MESH = pl.DeviceIdType.MESH
BF16 = jnp.bfloat16
F32 = jnp.float32
MIB = 1024 * 1024
PANEL = 16


def split2(x):
    hi = x.astype(BF16)
    lo = (x - hi.astype(F32)).astype(BF16)
    return hi, lo


def greet(peers):
    barrier = pltpu.get_barrier_semaphore()
    for cond, device in peers:
        if cond is None:
            pl.semaphore_signal(barrier, inc=1, device_id=device, device_id_type=MESH)
        else:
            @pl.when(cond)
            def _(device=device):
                pl.semaphore_signal(barrier, inc=1, device_id=device, device_id_type=MESH)
    total = 0
    for cond, _ in peers:
        total = total + (1 if cond is None else jnp.where(cond, 1, 0))
    pl.semaphore_wait(barrier, total)


def relay_kernel(n_rows, n_cols, chunks, ahead, own, halo, near_s, near_r, far_s, far_r, sib_s, sib_r):
    r = lax.axis_index("rows")
    c = lax.axis_index("cols")
    odd = lax.rem(r, 2)
    partner = r + 1 - 2 * odd
    fwd_to = r + 2 - 4 * odd
    far_from = r - 2 + 4 * odd
    can_fwd = (fwd_to >= 0) & (fwd_to < n_rows)
    has_far = (far_from >= 0) & (far_from < n_rows)
    part = own.shape[0] // n_cols
    size = part // chunks
    near_slot = 1 - odd
    far_slot = odd

    peers = [(None, (partner, c)), (can_fwd, (fwd_to, c)), (has_far, (far_from, c))]
    peers += [(None, (r, lax.rem(c + d, n_cols))) for d in range(1, n_cols)]
    greet(peers)

    def rows_of(i, col):
        return pl.ds(pl.multiple_of(col * part + i * size, size), size)

    def near(i):
        return pltpu.make_async_remote_copy(
            src_ref=own.at[rows_of(i, c)], dst_ref=halo.at[odd, rows_of(i, c)],
            send_sem=near_s.at[i], recv_sem=near_r.at[i], device_id=(partner, c), device_id_type=MESH)

    def near_in(i):
        return pltpu.make_async_remote_copy(
            src_ref=own.at[rows_of(i, c)], dst_ref=halo.at[near_slot, rows_of(i, c)],
            send_sem=near_s.at[i], recv_sem=near_r.at[i], device_id=(partner, c), device_id_type=MESH)

    def far(i):
        return pltpu.make_async_remote_copy(
            src_ref=halo.at[near_slot, rows_of(i, c)], dst_ref=halo.at[far_slot, rows_of(i, c)],
            send_sem=far_s.at[i], recv_sem=far_r.at[i], device_id=(fwd_to, c), device_id_type=MESH)

    def sib(i, kind, d):
        slot = near_slot if kind == 0 else far_slot
        k = (kind * (n_cols - 1) + d - 1) * chunks + i
        return pltpu.make_async_remote_copy(
            src_ref=halo.at[slot, rows_of(i, c)], dst_ref=halo.at[slot, rows_of(i, c)],
            send_sem=sib_s.at[k], recv_sem=sib_r.at[k],
            device_id=(r, lax.rem(c + d, n_cols)), device_id_type=MESH)

    def sib_in(i, kind, d):
        slot = near_slot if kind == 0 else far_slot
        k = (kind * (n_cols - 1) + d - 1) * chunks + i
        col = lax.rem(c + n_cols - d, n_cols)
        return pltpu.make_async_remote_copy(
            src_ref=halo.at[slot, rows_of(i, c)], dst_ref=halo.at[slot, rows_of(i, col)],
            send_sem=sib_s.at[k], recv_sem=sib_r.at[k],
            device_id=(r, lax.rem(c + d, n_cols)), device_id_type=MESH)

    for i in range(ahead):
        near(i).start()

    @pl.loop(0, chunks + 1)
    def _(i):
        @pl.when(i < chunks)
        def _():
            near_in(i).wait_recv()

            @pl.when(can_fwd)
            def _():
                far(i).start()

            for d in range(1, n_cols):
                sib(i, 0, d).start()

            @pl.when(i + ahead < chunks)
            def _():
                near(i + ahead).start()

        @pl.when((i > 0) & has_far)
        def _():
            far(i - 1).wait_recv()
            for d in range(1, n_cols):
                sib(i - 1, 1, d).start()

    @pl.loop(0, chunks)
    def _(i):
        for d in range(1, n_cols):
            sib_in(i, 0, d).wait_recv()
            sib(i, 0, d).wait_send()

        @pl.when(has_far)
        def _():
            for d in range(1, n_cols):
                sib_in(i, 1, d).wait_recv()
                sib(i, 1, d).wait_send()

        near(i).wait_send()

        @pl.when(can_fwd)
        def _():
            far(i).wait_send()


def relay(block_vector, n_rows, n_cols):
    rows, width = block_vector.shape
    chunks = 16
    dma = pltpu.SemaphoreType.DMA
    n_sib = max(1, 2 * (n_cols - 1) * chunks)
    return pl.pallas_call(
        functools.partial(relay_kernel, n_rows, n_cols, chunks, 4),
        out_shape=jax.ShapeDtypeStruct((2, rows, width), F32),
        in_specs=[pl.BlockSpec(memory_space=pl.ANY)],
        out_specs=pl.BlockSpec(memory_space=pl.ANY),
        scratch_shapes=[dma((chunks,)), dma((chunks,)), dma((chunks,)), dma((chunks,)), dma((n_sib,)), dma((n_sib,))],
        compiler_params=pltpu.CompilerParams(collective_id=0, has_side_effects=True),
        name="halo_relay",
    )(block_vector)


def product_kernel(group, place, cols, counts, own, halo, tiles, out, ext, sems):
    g = pl.program_id(0)
    rows = own.shape[0]
    slots = tiles.shape[1]
    size = tiles.shape[2]
    blocks = rows // size

    @pl.when(g == 0)
    def _():
        moves = [
            pltpu.make_async_copy(halo.at[0], ext.at[pl.ds(0, rows)], sems.at[0]),
            pltpu.make_async_copy(own, ext.at[pl.ds(rows, rows)], sems.at[1]),
            pltpu.make_async_copy(halo.at[1], ext.at[pl.ds(2 * rows, rows)], sems.at[2]),
        ]
        for m in moves:
            m.start()
        for m in moves:
            m.wait()

    first_block = (place[0] - 1) * blocks
    first_slot = place[1] * slots

    @pl.loop(0, group)
    def _(j):
        row = g * group + j
        live = counts[row] - first_slot
        where = pl.ds(pl.multiple_of(j * size, size), size)

        @pl.when(live <= 0)
        def _():
            out[where, :] = jnp.zeros((size, out.shape[1]), F32)

        @pl.when(live > 0)
        def _():
            a_parts = []
            b_parts = []
            for s in range(slots):
                at = jnp.clip(cols[row, s] - first_block, 0, 3 * blocks - 1)
                b = ext[pl.ds(pl.multiple_of(at * size, size), size), :]
                b_parts.append(jnp.where(s < live, b, 0.0))
                a_parts.append(tiles[j, s])
            a_hi, a_lo = split2(jnp.concatenate(a_parts, axis=1))
            b_hi, b_lo = split2(jnp.concatenate(b_parts, axis=0))
            both = jnp.dot(a_hi, jnp.concatenate([b_hi, b_lo], axis=1), preferred_element_type=F32)
            rest = jnp.dot(a_lo, b_hi, preferred_element_type=F32)
            width = out.shape[1]
            out[where, :] = both[:, :width] + both[:, width:] + rest


def products(place, tile_cols, live_counts, block_vector, halo, op_tiles):
    blocks, slots, size, _ = op_tiles.shape
    rows, width = block_vector.shape
    group = 4
    return pl.pallas_call(
        functools.partial(product_kernel, group),
        out_shape=jax.ShapeDtypeStruct((rows, width), F32),
        grid_spec=pltpu.PrefetchScalarGridSpec(
            num_scalar_prefetch=3,
            grid=(blocks // group,),
            in_specs=[
                pl.BlockSpec(memory_space=pl.ANY),
                pl.BlockSpec(memory_space=pl.ANY),
                pl.BlockSpec((group, slots, size, size), lambda g, *_: (g, 0, 0, 0)),
            ],
            out_specs=pl.BlockSpec((group * size, width), lambda g, *_: (g, 0)),
            scratch_shapes=[pltpu.VMEM((3 * rows, width), F32), pltpu.SemaphoreType.DMA((3,))],
        ),
        compiler_params=pltpu.CompilerParams(vmem_limit_bytes=40 * MIB),
        name="tile_products",
    )(place, tile_cols, live_counts, block_vector, halo, op_tiles)


def gram_kernel(n_rows, n_cols, chunks, partial, rows_out, gram_out, got, acc, into, part_s, part_r, sum_s, sum_r):
    r = lax.axis_index("rows")
    c = lax.axis_index("cols")
    part = partial.shape[0] // n_cols
    size = part // chunks
    steps = int(math.log2(n_rows))
    width = partial.shape[1]

    peers = [(None, (r, lax.rem(c + d, n_cols))) for d in range(1, n_cols)]
    row_peers = []
    for s in range(steps):
        bit = lax.rem(r // (1 << s), 2)
        row_peers.append(r + (1 << s) * (1 - 2 * bit))
    peers += [(None, (p, c)) for p in row_peers]
    greet(peers)

    def give(i, d):
        to = lax.rem(c + d, n_cols)
        src = pl.ds(pl.multiple_of(to * part + i * size, size), size)
        dst = pl.ds(pl.multiple_of(i * size, size), size)
        k = (d - 1) * chunks + i
        return pltpu.make_async_remote_copy(
            src_ref=partial.at[src], dst_ref=got.at[d - 1, dst], send_sem=part_s.at[k], recv_sem=part_r.at[k],
            device_id=(r, to), device_id_type=MESH)

    @pl.loop(0, chunks)
    def _(i):
        for d in range(1, n_cols):
            give(i, d).start()

    acc[0] = jnp.zeros_like(acc.at[0])

    @pl.loop(0, chunks)
    def _(i):
        here = pl.ds(pl.multiple_of(i * size, size), size)
        x = partial[pl.ds(pl.multiple_of(c * part + i * size, size), size), :]
        for d in range(1, n_cols):
            give(i, d).wait_recv()
            x = x + got[d - 1, here, :]
        rows_out[here, :] = x
        hi, lo = split2(x)
        both = jnp.concatenate([hi, lo], axis=1)
        g = lax.dot_general(both, both, (((0,), (0,)), ((), ())), preferred_element_type=F32)
        acc[0] += (g[:width, :width] + g[width:, width:]) + (g[:width, width:] + g[width:, :width])

    def add_up(s, k, device):
        return pltpu.make_async_remote_copy(
            src_ref=acc.at[s], dst_ref=into.at[k], send_sem=sum_s.at[k], recv_sem=sum_r.at[k],
            device_id=device, device_id_type=MESH)

    sent = []
    s = 0
    if n_cols == 2:
        sent.append(add_up(0, 0, (r, 1 - c)))
        sent[-1].start()
        sent[-1].wait_recv()
        acc[1] = acc[0] + into[0]
        s = 1
    elif n_cols > 2:
        bits = int(math.log2(n_cols))
        for b in range(bits):
            bit = lax.rem(c // (1 << b), 2)
            sent.append(add_up(s, s, (r, c + (1 << b) * (1 - 2 * bit))))
            sent[-1].start()
            sent[-1].wait_recv()
            acc[s + 1] = acc[s] + into[s]
            s += 1
    for p in row_peers:
        sent.append(add_up(s, s, (p, c)))
        sent[-1].start()
        sent[-1].wait_recv()
        acc[s + 1] = acc[s] + into[s]
        s += 1
    gram_out[...] = acc[s]
    for copy in sent:
        copy.wait_send()

    @pl.loop(0, chunks)
    def _(i):
        for d in range(1, n_cols):
            give(i, d).wait_send()


def rows_and_gram(partial, n_rows, n_cols):
    rows, width = partial.shape
    part = rows // n_cols
    chunks = 4
    steps = int(math.log2(n_rows * n_cols))
    n_give = max(1, (n_cols - 1) * chunks)
    dma = pltpu.SemaphoreType.DMA
    vmem = pl.BlockSpec(memory_space=pltpu.VMEM)
    return pl.pallas_call(
        functools.partial(gram_kernel, n_rows, n_cols, chunks),
        out_shape=(jax.ShapeDtypeStruct((part, width), F32), jax.ShapeDtypeStruct((width, width), F32)),
        in_specs=[vmem],
        out_specs=(vmem, vmem),
        scratch_shapes=[
            pltpu.VMEM((max(1, n_cols - 1), part, width), F32),
            pltpu.VMEM((steps + 1, width, width), F32),
            pltpu.VMEM((max(1, steps), width, width), F32),
            dma((n_give,)), dma((n_give,)), dma((max(1, steps),)), dma((max(1, steps),)),
        ],
        compiler_params=pltpu.CompilerParams(collective_id=1, has_side_effects=True, vmem_limit_bytes=40 * MIB),
        name="rows_and_gram",
    )(partial)


def spread(x):
    x1 = x.astype(BF16).astype(F32)
    x2 = (x - x1).astype(BF16).astype(F32)
    return x1, x2, x - x1 - x2


def factor(gram):
    n = gram.shape[0]
    nb = PANEL
    lane = lax.broadcasted_iota(jnp.int32, (nb, n), 1)
    sub = lax.broadcasted_iota(jnp.int32, (nb, n), 0)
    eye = (lax.broadcasted_iota(jnp.int32, (n, n), 0) == lax.broadcasted_iota(jnp.int32, (n, n), 1)).astype(F32)
    left, right = gram, eye
    upper, inverse = [], []
    for p in range(n // nb):
        a = left[:nb]
        w = right[:nb]
        cols = [jnp.broadcast_to(a[:, p * nb + k:p * nb + k + 1], (nb, n)) for k in range(nb)]
        for j in range(nb):
            scale = lax.rsqrt(jnp.broadcast_to(cols[j][j:j + 1], (nb, n)))
            col = cols[j] * scale
            below = jnp.where(sub > j, col, 0.0)
            for k in range(j + 1, nb):
                cols[k] = cols[k] - below * jnp.broadcast_to(col[k:k + 1], (nb, n))
            a_row = jnp.broadcast_to(a[j:j + 1], (nb, n)) * scale
            w_row = jnp.broadcast_to(w[j:j + 1], (nb, n)) * scale
            a = jnp.where(sub == j, a_row, a - below * a_row)
            w = jnp.where(sub == j, w_row, w - below * w_row)
        upper.append(jnp.where(lane >= sub + p * nb, a, 0.0))
        inverse.append(w)
        rest = n - (p + 1) * nb
        if rest:
            a1, a2, a3 = spread(a)
            w1, w2, w3 = spread(w)
            lhs = jnp.concatenate([a1, a1, a2, a1, a2, a3], axis=0).T[n - rest:].astype(BF16)
            rhs_a = jnp.concatenate([a1, a2, a1, a3, a2, a1], axis=0)
            rhs_w = jnp.concatenate([w1, w2, w1, w3, w2, w1], axis=0)
            rhs = jnp.concatenate([rhs_a, rhs_w], axis=1).astype(BF16)
            change = jnp.dot(lhs, rhs, preferred_element_type=F32)
            left = left[nb:] - change[:, :n]
            right = right[nb:] - change[:, n:]
    return jnp.concatenate(upper, axis=0), jnp.concatenate(inverse, axis=0)


def basis_kernel(root, gram, rows, basis, r_factor, solve):
    @pl.when(pl.program_id(0) == 0)
    def _():
        upper, inverse = factor(gram[...])
        r_factor[...] = upper / root
        solve[...] = inverse * root

    width = rows.shape[1]
    x_hi, x_lo = split2(rows[...])
    s_hi, s_lo = split2(solve[...])
    both = lax.dot_general(x_hi, jnp.concatenate([s_hi, s_lo], axis=0), (((1,), (1,)), ((), ())),
                           preferred_element_type=F32)
    rest = lax.dot_general(x_lo, s_hi, (((1,), (1,)), ((), ())), preferred_element_type=F32)
    basis[...] = both[:, :width] + both[:, width:] + rest


def basis_of(gram, rows, root):
    part, width = rows.shape
    size = min(part, 1024)
    return pl.pallas_call(
        functools.partial(basis_kernel, root),
        out_shape=(jax.ShapeDtypeStruct((part, width), F32), jax.ShapeDtypeStruct((width, width), F32)),
        grid=(part // size,),
        in_specs=[
            pl.BlockSpec((width, width), lambda i: (0, 0)),
            pl.BlockSpec((size, width), lambda i: (i, 0)),
        ],
        out_specs=(
            pl.BlockSpec((size, width), lambda i: (i, 0)),
            pl.BlockSpec((width, width), lambda i: (0, 0)),
        ),
        scratch_shapes=[pltpu.VMEM((width, width), F32)],
        compiler_params=pltpu.CompilerParams(vmem_limit_bytes=24 * MIB),
        name="factor_and_basis",
    )(gram, rows)


def on_device(n_rows, n_cols, block_vector, op_tiles, tile_cols, live_counts):
    place = jnp.stack([lax.axis_index("rows"), lax.axis_index("cols")]).astype(jnp.int32)
    halo = relay(block_vector, n_rows, n_cols)
    partial = products(place, tile_cols, live_counts, block_vector, halo, op_tiles)
    rows, gram = rows_and_gram(partial, n_rows, n_cols)
    root = math.sqrt(block_vector.shape[0] * n_rows)
    return basis_of(gram, rows, root)


def solution(mesh):
    in_specs = (P("rows", None), P("rows", "cols", None, None), P("rows", "cols"), P("rows"))
    out_specs = (P(("rows", "cols"), None), P())
    return jax.shard_map(
        functools.partial(on_device, mesh.shape["rows"], mesh.shape["cols"]),
        mesh=mesh, in_specs=in_specs, out_specs=out_specs, check_vma=False,
    )
```

time: 423 us -> 115 us (0.27)
  the two profiles are of different devices: /device:TPU:2 before, /device:TPU:0 now
where the time goes in v1:
time: 115 us
  Pallas kernels  111 us (97%)
  local copies, waits for them, and re-layouts  2.96 us (3%)
    pallas_call x1, Pallas kernels, relay(): pl.pallas_call(functools.partial(relay_kernel, n_rows, n_cols, chunks, 4)...  55.2 us
    pallas_call x1, Pallas kernels, rows_and_gram(): pl.pallas_call(functools.partial(gram_kernel, n_rows, n_cols, chunks), ou...  25.7 us
    pallas_call x1, Pallas kernels, products(): pl.pallas_call(functools.partial(product_kernel, group), out_shape=jax.Sh...  23.7 us
    pallas_call x1, Pallas kernels, basis_of(): pl.pallas_call(functools.partial(basis_kernel, root), out_shape=(jax.Shap...  6.36 us
    unnamed x5, local copies, waits for them, and re-layouts  2.96 us

profile of v1, /device:TPU:0, one launch (start us, length us, event | category | flops | bytes accessed | tf_op | source)
XLA Modules:
  0.0 114.6 jit_solution(2878083835307791524)
XLA Ops:
  0.6 0.1 pad_add_fusion.place
  0.7 0.8 copy.6.cols
  1.5 0.0 copy-start.1
  1.5 55.2 %halo_relay.1.halo = f32[2,8192,128]{2,1,0:T(8,128)} custom-call(f32[8192,128]{1,0:T(8,128)} %own.3), custom_call_target="tpu_custom_call" | custom-call | tf_op jit(solution)/shard_map/halo_relay/pallas_call | solution.py:142
  56.7 0.0 copy-done.1
  56.7 0.0 copy-start
  56.7 2.2 %copy-done = f32[8192,128]{1,0:T(8,128)S(1)} copy-done((f32[8192,128]{1,0:T(8,128)S(1)}, f32[8192,128]{1,0:T(8,128)}, u32[]{:S(2)}) %copy-start) | copy-done | bytes 4194328
  58.9 23.7 %tile_products.1.partial = f32[8192,128]{1,0:T(8,128)S(1)} custom-call(s32[2]{0:T(128)S(1)} %pad_add_fusion.place, s32[64,4]{1,0:T(8,128)S(1)} %copy.6.cols, s32[64]{0:T(128)S(1)} %copy-done.1, f32[8192,128]{1,0:T(8,128)S(1)} %copy-done, f32[2,8192,128]{2,1,0:T(8,128)} %halo_relay.1.halo, f32[64,4,128,128]{3,2,1,0:T(8,128)} %tiles.1), custom_call_target="tpu_custom_call" | custom-call | tf_op jit(solution)/shard_map/tile_products/pallas_call | solution.py:206
  82.6 25.7 %rows_and_gram.1 = (f32[4096,128]{1,0:T(8,128)S(1)}, f32[128,128]{1,0:T(8,128)S(1)}) custom-call(f32[8192,128]{1,0:T(8,128)S(1)} %tile_products.1.partial), custom_call_target="tpu_custom_call" | custom-call | tf_op jit(solution)/shard_map/rows_and_gram/pallas_call | solution.py:316
  108.3 6.4 %factor_and_basis.1 = (f32[4096,128]{1,0:T(8,128)}, f32[128,128]{1,0:T(8,128)}) custom-call(f32[128,128]{1,0:T(8,128)S(1)} %get-tuple-element.4.gram, f32[4096,128]{1,0:T(8,128)S(1)} %get-tuple-element.5.rows), custom_call_target="tpu_custom_call" | custom-call | tf_op jit(solution)/shard_map/factor_and_basis/pallas_call | solution.py:395
Async XLA Ops:
  1.5 55.2 %copy-start.1 = (s32[64]{0:T(128)S(1)}, s32[64]{0:T(128)}, u32[]{:S(2)}) copy-start(s32[64]{0:T(128)} %counts.1) | copy-start | bytes 772
  56.7 2.2 %copy-start = (f32[8192,128]{1,0:T(8,128)S(1)}, f32[8192,128]{1,0:T(8,128)}, u32[]{:S(2)}) copy-start(f32[8192,128]{1,0:T(8,128)} %own.3) | copy-start | bytes 12582916

commit v2 on v1

v2 whole, which is shorter than its diff:
```python
import functools
import math

import jax
import jax.numpy as jnp
from jax import lax
from jax.experimental import pallas as pl
from jax.experimental.pallas import tpu as pltpu
from jax.sharding import PartitionSpec as P

MESH = pl.DeviceIdType.MESH
BF16 = jnp.bfloat16
F32 = jnp.float32
MIB = 1024 * 1024
PANEL = 16


def split2(x):
    hi = x.astype(BF16)
    lo = (x - hi.astype(F32)).astype(BF16)
    return hi, lo


def greet(peers):
    barrier = pltpu.get_barrier_semaphore()
    for cond, device in peers:
        if cond is None:
            pl.semaphore_signal(barrier, inc=1, device_id=device, device_id_type=MESH)
        else:
            @pl.when(cond)
            def _(device=device):
                pl.semaphore_signal(barrier, inc=1, device_id=device, device_id_type=MESH)
    total = 0
    for cond, _ in peers:
        total = total + (1 if cond is None else jnp.where(cond, 1, 0))
    pl.semaphore_wait(barrier, total)


def step_kernel(n_rows, n_cols, chunks, ahead, lag, pieces, cols, counts, own, tiles, rows_out, gram_out,
                own_v, halo, stage, a_hi, a_lo, out, got, acc, into,
                own_sem, stage_sem, rows_sem, near_s, near_r, far_s, far_r, sib_s, sib_r, part_s, part_r, sum_s, sum_r):
    r = lax.axis_index("rows")
    c = lax.axis_index("cols")
    blocks, slots, tile, _ = tiles.shape
    rows, width = blocks * tile, own.shape[2]
    odd = lax.rem(r, 2)
    partner = r + 1 - 2 * odd
    fwd_to = r + 2 - 4 * odd
    far_from = r - 2 + 4 * odd
    can_fwd = (fwd_to >= 0) & (fwd_to < n_rows)
    has_far = (far_from >= 0) & (far_from < n_rows)
    part = rows // n_cols
    size = part // chunks
    near_slot = 1 - odd
    far_slot = odd
    siblings = [(r, lax.rem(c + d, n_cols)) for d in range(1, n_cols)]
    steps = int(math.log2(n_rows))
    sum_peers = []
    for b in range(int(math.log2(n_cols))):
        bit = lax.rem(c // (1 << b), 2)
        sum_peers.append((r, c + (1 << b) * (1 - 2 * bit)))
    for b in range(steps):
        bit = lax.rem(r // (1 << b), 2)
        sum_peers.append((r + (1 << b) * (1 - 2 * bit), c))

    peers = [(None, (partner, c)), (can_fwd, (fwd_to, c)), (has_far, (far_from, c))]
    peers += [(None, device) for device in siblings]
    peers += [(None, device) for device in sum_peers[int(math.log2(n_cols)) + 1:]]

    def remote(src, dst, send_sem, recv_sem, device):
        return pltpu.make_async_remote_copy(
            src_ref=src, dst_ref=dst, send_sem=send_sem, recv_sem=recv_sem, device_id=device, device_id_type=MESH)

    def own_at(i, col):
        row = col * part + i * size
        return own.at[row // tile, pl.ds(pl.multiple_of(lax.rem(row, tile), size), size)]

    def halo_at(slot, i, col):
        row = col * part + i * size
        return halo.at[slot * blocks + row // tile, pl.ds(pl.multiple_of(lax.rem(row, tile), size), size)]

    def near(i):
        return remote(own_at(i, c), halo_at(odd, i, c), near_s.at[i], near_r.at[i], (partner, c))

    def near_in(i):
        return remote(own_at(i, c), halo_at(near_slot, i, c), near_s.at[i], near_r.at[i], (partner, c))

    def far(i):
        return remote(halo_at(near_slot, i, c), halo_at(far_slot, i, c),
                      far_s.at[i], far_r.at[i], (fwd_to, c))

    def sib(i, kind, d, incoming=False):
        slot = near_slot if kind == 0 else far_slot
        k = (kind * (n_cols - 1) + d - 1) * chunks + i
        col = lax.rem(c + n_cols - d, n_cols) if incoming else c
        return remote(halo_at(slot, i, c), halo_at(slot, i, col),
                      sib_s.at[k], sib_r.at[k], siblings[d - 1])

    group = blocks // chunks

    def fetch(i):
        k = lax.rem(i, 2)
        return pltpu.make_async_copy(tiles.at[pl.ds(i * group, group)], stage.at[k], stage_sem.at[k])

    bring_own = pltpu.make_async_copy(own, own_v, own_sem)
    bring_own.start()
    fetch(0).start()
    greet(peers)
    for i in range(ahead):
        near(i).start()

    before = (r - 1) * blocks
    first_slot = c * slots

    def picked(row, ours):
        live = counts[row] - first_slot
        parts = []
        for s in range(slots):
            rel = cols[row, s] - before
            after_prev = (rel >= blocks).astype(jnp.int32)
            after_own = (rel >= 2 * blocks).astype(jnp.int32)
            mine = after_prev - after_own
            alive = (live > s).astype(jnp.int32)
            if ours:
                use = mine * alive
                at = use * (rel - blocks)
                b = own_v[lax.max(lax.min(at, blocks - 1), 0)]
            else:
                use = (1 - mine) * alive
                at = use * (rel - blocks * after_own) + (1 - use) * (near_slot * blocks)
                b = halo[lax.max(lax.min(at, 2 * blocks - 1), 0)]
            parts.append(b * use.astype(F32))
        return split2(jnp.concatenate(parts, axis=0))

    def times(hi, lo, b_hi, b_lo):
        both = jnp.dot(hi, jnp.concatenate([b_hi, b_lo], axis=1), preferred_element_type=F32)
        return both[:, :width] + both[:, width:] + jnp.dot(lo, b_hi, preferred_element_type=F32)

    def at_block(row):
        return pl.ds(pl.multiple_of(row * tile, tile), tile)

    def own_products(i):
        k = lax.rem(i, 2)
        fetch(i).wait()

        @pl.when(i + 1 < chunks)
        def _():
            fetch(i + 1).start()

        for j in range(group):
            row = i * group + j
            hi, lo = split2(jnp.concatenate([stage[k, j, s] for s in range(slots)], axis=1))
            a_hi[row] = hi
            a_lo[row] = lo
            b_hi, b_lo = picked(row, True)
            out[at_block(row), :] = times(hi, lo, b_hi, b_lo)

    def halo_products(at_rows):
        sums = []
        for row in at_rows:
            b_hi, b_lo = picked(row, False)
            sums.append(out[at_block(row), :] + times(a_hi[row], a_lo[row], b_hi, b_lo))
        for row, total in zip(at_rows, sums):
            out[at_block(row), :] = total

    @pl.loop(0, chunks + lag)
    def _(i):
        @pl.when(i < chunks)
        def _():
            near_in(i).wait_recv()

            @pl.when(can_fwd)
            def _():
                far(i).start()

            for d in range(1, n_cols):
                sib(i, 0, d).start()

            @pl.when(i + ahead < chunks)
            def _():
                near(i + ahead).start()

        @pl.when((i >= lag) & has_far)
        def _():
            far(i - lag).wait_recv()
            for d in range(1, n_cols):
                sib(i - lag, 1, d).start()

        @pl.when(i == 0)
        def _():
            bring_own.wait()

        @pl.when(i < chunks)
        def _():
            own_products(i)

    @pl.loop(0, chunks)
    def _(i):
        for d in range(1, n_cols):
            sib(i, 0, d, True).wait_recv()
            sib(i, 0, d).wait_send()

        @pl.when(has_far)
        def _():
            for d in range(1, n_cols):
                sib(i, 1, d, True).wait_recv()
                sib(i, 1, d).wait_send()

        near(i).wait_send()

        @pl.when(can_fwd)
        def _():
            far(i).wait_send()

    piece = part // pieces
    piece_blocks = piece // tile
    unroll = 2 if piece_blocks % 2 == 0 else 1

    def multiply_piece(col, i):
        first = col * (part // tile) + i * piece_blocks

        @pl.loop(0, piece_blocks // unroll)
        def _(j):
            halo_products([first + j * unroll + u for u in range(unroll)])

    def piece_span(col, i):
        return pl.ds(pl.multiple_of(col * part + i * piece, piece), piece)

    def give(i, d):
        k = (d - 1) * pieces + i
        return remote(out.at[piece_span(lax.rem(c + d, n_cols), i)], got.at[d - 1, piece_span(0, i)],
                      part_s.at[k], part_r.at[k], siblings[d - 1])

    def keep(i):
        return pltpu.make_async_copy(out.at[piece_span(c, i)], rows_out.at[piece_span(0, i)], rows_sem.at[i])

    for d in range(1, n_cols):
        @pl.loop(0, pieces)
        def _(i, d=d):
            multiply_piece(lax.rem(c + d, n_cols), i)
            give(i, d).start()

    acc[0] = jnp.zeros_like(acc.at[0])

    @pl.loop(0, pieces)
    def _(i):
        multiply_piece(c, i)
        x = out[piece_span(c, i), :]
        for d in range(1, n_cols):
            give(i, d).wait_recv()
            x = x + got[d - 1, piece_span(0, i), :]
        out[piece_span(c, i), :] = x
        keep(i).start()
        hi, lo = split2(x)
        both = jnp.concatenate([hi, lo], axis=1)
        g = lax.dot_general(both, both, (((0,), (0,)), ((), ())), preferred_element_type=F32)
        acc[0] += (g[:width, :width] + g[width:, width:]) + (g[:width, width:] + g[width:, :width])

    def add_up(s):
        return remote(acc.at[s], into.at[s], sum_s.at[s], sum_r.at[s], sum_peers[s])

    for s in range(len(sum_peers)):
        add_up(s).start()
        add_up(s).wait_recv()
        acc[s + 1] = acc[s] + into[s]
    gram_out[...] = acc[len(sum_peers)]

    for s in range(len(sum_peers)):
        add_up(s).wait_send()

    @pl.loop(0, pieces)
    def _(i):
        keep(i).wait()
        for d in range(1, n_cols):
            give(i, d).wait_send()


def rows_and_gram(tile_cols, live_counts, block_vector, op_tiles, n_rows, n_cols):
    rows, width = block_vector.shape
    blocks, slots, tile, _ = op_tiles.shape
    part = rows // n_cols
    chunks = min(32, blocks)
    while part // chunks > tile:
        chunks *= 2
    pieces = 4
    sums = int(math.log2(n_rows * n_cols))
    n_sib = max(1, 2 * (n_cols - 1) * chunks)
    n_give = max(1, (n_cols - 1) * pieces)
    dma = pltpu.SemaphoreType.DMA
    vmem = pl.BlockSpec(memory_space=pltpu.VMEM)
    smem = pl.BlockSpec(memory_space=pltpu.SMEM)
    hbm = pl.BlockSpec(memory_space=pl.ANY)
    return pl.pallas_call(
        functools.partial(step_kernel, n_rows, n_cols, chunks, 8, 2, pieces),
        out_shape=(jax.ShapeDtypeStruct((part, width), F32), jax.ShapeDtypeStruct((width, width), F32)),
        in_specs=[smem, smem, hbm, hbm],
        out_specs=(hbm, vmem),
        scratch_shapes=[
            pltpu.VMEM((blocks, tile, width), F32),
            pltpu.VMEM((2 * blocks, tile, width), F32),
            pltpu.VMEM((2, blocks // chunks, slots, tile, tile), F32),
            pltpu.VMEM((blocks, tile, slots * tile), BF16),
            pltpu.VMEM((blocks, tile, slots * tile), BF16),
            pltpu.VMEM((rows, width), F32),
            pltpu.VMEM((max(1, n_cols - 1), part, width), F32),
            pltpu.VMEM((sums + 1, width, width), F32),
            pltpu.VMEM((sums, width, width), F32),
            dma, dma((2,)), dma((pieces,)),
            dma((chunks,)), dma((chunks,)), dma((chunks,)), dma((chunks,)), dma((n_sib,)), dma((n_sib,)),
            dma((n_give,)), dma((n_give,)), dma((sums,)), dma((sums,)),
        ],
        compiler_params=pltpu.CompilerParams(collective_id=0, has_side_effects=True, vmem_limit_bytes=48 * MIB),
        name="rows_and_gram",
    )(tile_cols, live_counts, block_vector.reshape(blocks, tile, width), op_tiles)


def spread(x):
    x1 = x.astype(BF16).astype(F32)
    x2 = (x - x1).astype(BF16).astype(F32)
    return x1, x2, x - x1 - x2


def factor(gram):
    n = gram.shape[0]
    nb = PANEL
    lane = lax.broadcasted_iota(jnp.int32, (nb, n), 1)
    sub = lax.broadcasted_iota(jnp.int32, (nb, n), 0)
    eye = (lax.broadcasted_iota(jnp.int32, (n, n), 0) == lax.broadcasted_iota(jnp.int32, (n, n), 1)).astype(F32)
    left, right = gram, eye
    upper, inverse = [], []
    for p in range(n // nb):
        a = left[:nb]
        w = right[:nb]
        cols = [jnp.broadcast_to(a[:, p * nb + k:p * nb + k + 1], (nb, n)) for k in range(nb)]
        for j in range(nb):
            scale = lax.rsqrt(jnp.broadcast_to(cols[j][j:j + 1], (nb, n)))
            col = cols[j] * scale
            below = jnp.where(sub > j, col, 0.0)
            for k in range(j + 1, nb):
                cols[k] = cols[k] - below * jnp.broadcast_to(col[k:k + 1], (nb, n))
            a_row = jnp.broadcast_to(a[j:j + 1], (nb, n)) * scale
            w_row = jnp.broadcast_to(w[j:j + 1], (nb, n)) * scale
            a = jnp.where(sub == j, a_row, a - below * a_row)
            w = jnp.where(sub == j, w_row, w - below * w_row)
        upper.append(jnp.where(lane >= sub + p * nb, a, 0.0))
        inverse.append(w)
        rest = n - (p + 1) * nb
        if rest:
            a1, a2, a3 = spread(a)
            w1, w2, w3 = spread(w)
            lhs = jnp.concatenate([a1, a1, a2, a1, a2, a3], axis=0).T[n - rest:].astype(BF16)
            rhs_a = jnp.concatenate([a1, a2, a1, a3, a2, a1], axis=0)
            rhs_w = jnp.concatenate([w1, w2, w1, w3, w2, w1], axis=0)
            rhs = jnp.concatenate([rhs_a, rhs_w], axis=1).astype(BF16)
            change = jnp.dot(lhs, rhs, preferred_element_type=F32)
            left = left[nb:] - change[:, :n]
            right = right[nb:] - change[:, n:]
    return jnp.concatenate(upper, axis=0), jnp.concatenate(inverse, axis=0)


def basis_kernel(root, gram, rows, basis, r_factor, solve):
    @pl.when(pl.program_id(0) == 0)
    def _():
        upper, inverse = factor(gram[...])
        r_factor[...] = upper / root
        solve[...] = inverse * root

    width = rows.shape[1]
    x_hi, x_lo = split2(rows[...])
    s_hi, s_lo = split2(solve[...])
    both = lax.dot_general(x_hi, jnp.concatenate([s_hi, s_lo], axis=0), (((1,), (1,)), ((), ())),
                           preferred_element_type=F32)
    rest = lax.dot_general(x_lo, s_hi, (((1,), (1,)), ((), ())), preferred_element_type=F32)
    basis[...] = both[:, :width] + both[:, width:] + rest


def basis_of(gram, rows, root):
    part, width = rows.shape
    size = min(part, 1024)
    return pl.pallas_call(
        functools.partial(basis_kernel, root),
        out_shape=(jax.ShapeDtypeStruct((part, width), F32), jax.ShapeDtypeStruct((width, width), F32)),
        grid=(part // size,),
        in_specs=[
            pl.BlockSpec((width, width), lambda i: (0, 0)),
            pl.BlockSpec((size, width), lambda i: (i, 0)),
        ],
        out_specs=(
            pl.BlockSpec((size, width), lambda i: (i, 0)),
            pl.BlockSpec((width, width), lambda i: (0, 0)),
        ),
        scratch_shapes=[pltpu.VMEM((width, width), F32)],
        compiler_params=pltpu.CompilerParams(vmem_limit_bytes=24 * MIB),
        name="factor_and_basis",
    )(gram, rows)


def on_device(n_rows, n_cols, block_vector, op_tiles, tile_cols, live_counts):
    rows, gram = rows_and_gram(tile_cols, live_counts, block_vector, op_tiles, n_rows, n_cols)
    root = math.sqrt(block_vector.shape[0] * n_rows)
    return basis_of(gram, rows, root)


def solution(mesh):
    in_specs = (P("rows", None), P("rows", "cols", None, None), P("rows", "cols"), P("rows"))
    out_specs = (P(("rows", "cols"), None), P())
    return jax.shard_map(
        functools.partial(on_device, mesh.shape["rows"], mesh.shape["cols"]),
        mesh=mesh, in_specs=in_specs, out_specs=out_specs, check_vma=False,
    )
```

time: 115 us -> 94.9 us (0.83)
  the two profiles are of different devices: /device:TPU:0 before, /device:TPU:2 now
where the time goes in v2:
time: 94.9 us; the launch traced here: 94.6 us
  Pallas kernels  92.6 us (98%)
  local copies, waits for them, and re-layouts  1.43 us (2%)
    pallas_call x1, Pallas kernels, rows_and_gram(): pl.pallas_call(functools.partial(step_kernel, n_rows, n_cols, chunks, 8,...  86.2 us
    pallas_call x1, Pallas kernels, basis_of(): pl.pallas_call(functools.partial(basis_kernel, root), out_shape=(jax.Shap...  6.38 us

profile of v2, /device:TPU:2, one launch (start us, length us, event | category | flops | bytes accessed | tf_op | source)
XLA Modules:
  0.0 94.6 jit_solution(14326532141704240494)
XLA Ops:
  0.6 0.8 copy.6.cols
  1.4 0.0 copy-start
  1.4 0.7 copy-done
  2.1 86.2 %rows_and_gram.1 = (f32[4096,128]{1,0:T(8,128)S(1)}, f32[128,128]{1,0:T(8,128)S(1)}) custom-call(s32[64,4]{1,0:T(8,128)S(1)} %copy.6.cols, s32[64]{0:T(128)S(1)} %copy-done, f32[64,128,128]{2,1,0:T(8,128)} %bitcast.1, f32[64,4,128,128]{3,2,1,0:T(8,128)} %tiles.1), custom_call_target="tpu_custom_call" | custom-call | tf_op jit(solution)/shard_map/rows_and_gram/pallas_call | solution.py:293
  88.3 6.4 %factor_and_basis.1 = (f32[4096,128]{1,0:T(8,128)}, f32[128,128]{1,0:T(8,128)}) custom-call(f32[128,128]{1,0:T(8,128)S(1)} %get-tuple-element.4.gram, f32[4096,128]{1,0:T(8,128)S(1)} %get-tuple-element.5.rows), custom_call_target="tpu_custom_call" | custom-call | tf_op jit(solution)/shard_map/factor_and_basis/pallas_call | solution.py:380
Async XLA Ops:
  1.4 0.7 copy-start

commit v3 on v2

--- a/solution.py
+++ b/solution.py
@@ -37,8 +37,9 @@
 
 
 def step_kernel(n_rows, n_cols, chunks, ahead, lag, pieces, cols, counts, own, tiles, rows_out, gram_out,
-                own_v, halo, stage, a_hi, a_lo, out, got, acc, into,
-                own_sem, stage_sem, rows_sem, near_s, near_r, far_s, far_r, sib_s, sib_r, part_s, part_r, sum_s, sum_r):
+                own_v, own_split, halo, halo_split, stage, a_split, out, got, gram, halves, acc, into, full,
+                own_sem, stage_sem, rows_sem, near_s, near_r, far_s, far_r, sib_s, sib_r, part_s, part_r,
+                half_s, half_r, sum_s, sum_r, full_s, full_r):
     r = lax.axis_index("rows")
     c = lax.axis_index("cols")
     blocks, slots, tile, _ = tiles.shape
@@ -50,51 +51,55 @@
     can_fwd = (fwd_to >= 0) & (fwd_to < n_rows)
     has_far = (far_from >= 0) & (far_from < n_rows)
     part = rows // n_cols
+    part_blocks = part // tile
     size = part // chunks
     near_slot = 1 - odd
     far_slot = odd
     siblings = [(r, lax.rem(c + d, n_cols)) for d in range(1, n_cols)]
-    steps = int(math.log2(n_rows))
     sum_peers = []
-    for b in range(int(math.log2(n_cols))):
-        bit = lax.rem(c // (1 << b), 2)
-        sum_peers.append((r, c + (1 << b) * (1 - 2 * bit)))
-    for b in range(steps):
+    for b in range(int(math.log2(n_rows))):
         bit = lax.rem(r // (1 << b), 2)
         sum_peers.append((r + (1 << b) * (1 - 2 * bit), c))
 
     peers = [(None, (partner, c)), (can_fwd, (fwd_to, c)), (has_far, (far_from, c))]
     peers += [(None, device) for device in siblings]
-    peers += [(None, device) for device in sum_peers[int(math.log2(n_cols)) + 1:]]
+    peers += [(None, device) for device in sum_peers[1:]]
 
     def remote(src, dst, send_sem, recv_sem, device):
         return pltpu.make_async_remote_copy(
             src_ref=src, dst_ref=dst, send_sem=send_sem, recv_sem=recv_sem, device_id=device, device_id_type=MESH)
 
+    def chunk_place(i, col):
+        row = col * part + i * size
+        return row // tile, pl.ds(pl.multiple_of(lax.rem(row, tile), size), size)
+
     def own_at(i, col):
-        row = col * part + i * size
-        return own.at[row // tile, pl.ds(pl.multiple_of(lax.rem(row, tile), size), size)]
+        block, span = chunk_place(i, col)
+        return own.at[block, span]
 
     def halo_at(slot, i, col):
-        row = col * part + i * size
-        return halo.at[slot * blocks + row // tile, pl.ds(pl.multiple_of(lax.rem(row, tile), size), size)]
+        block, span = chunk_place(i, col)
+        return halo.at[slot * blocks + block, span]
 
     def near(i):
-        return remote(own_at(i, c), halo_at(odd, i, c), near_s.at[i], near_r.at[i], (partner, c))
+        return remote(own_at(i, c), halo_at(odd, i, c), near_s, near_r.at[i], (partner, c))
 
     def near_in(i):
-        return remote(own_at(i, c), halo_at(near_slot, i, c), near_s.at[i], near_r.at[i], (partner, c))
+        return remote(own_at(i, c), halo_at(near_slot, i, c), near_s, near_r.at[i], (partner, c))
 
     def far(i):
-        return remote(halo_at(near_slot, i, c), halo_at(far_slot, i, c),
-                      far_s.at[i], far_r.at[i], (fwd_to, c))
+        return remote(halo_at(near_slot, i, c), halo_at(far_slot, i, c), far_s, far_r.at[i], (fwd_to, c))
 
     def sib(i, kind, d, incoming=False):
         slot = near_slot if kind == 0 else far_slot
         k = (kind * (n_cols - 1) + d - 1) * chunks + i
         col = lax.rem(c + n_cols - d, n_cols) if incoming else c
         return remote(halo_at(slot, i, c), halo_at(slot, i, col),
-                      sib_s.at[k], sib_r.at[k], siblings[d - 1])
+                      sib_s.at[kind * (n_cols - 1) + d - 1], sib_r.at[k], siblings[d - 1])
+
+    def all_sent(sem, device):
+        whole = halo.at[pl.ds(near_slot * blocks + c * part_blocks, part_blocks)]
+        remote(whole, whole, sem, near_r.at[0], device).wait_send()
 
     group = blocks // chunks
 
@@ -109,6 +114,20 @@
     for i in range(ahead):
         near(i).start()
 
+    def split_halo(slot, i, col):
+        block, span = chunk_place(i, col)
+        hi, lo = split2(halo[slot * blocks + block, span, :])
+        halo_split[slot * blocks + block, span, :] = jnp.concatenate([hi, lo], axis=1)
+
+    own_split[blocks] = jnp.zeros((tile, 2 * width), BF16)
+    halo_split[2 * blocks] = jnp.zeros((tile, 2 * width), BF16)
+    bring_own.wait()
+
+    @pl.loop(0, blocks)
+    def _(i):
+        hi, lo = split2(own_v[i])
+        own_split[i] = jnp.concatenate([hi, lo], axis=1)
+
     before = (r - 1) * blocks
     first_slot = c * slots
 
@@ -116,25 +135,24 @@
         live = counts[row] - first_slot
         parts = []
         for s in range(slots):
-            rel = cols[row, s] - before
+            rel = cols[s, row] - before
             after_prev = (rel >= blocks).astype(jnp.int32)
             after_own = (rel >= 2 * blocks).astype(jnp.int32)
             mine = after_prev - after_own
             alive = (live > s).astype(jnp.int32)
             if ours:
                 use = mine * alive
-                at = use * (rel - blocks)
-                b = own_v[lax.max(lax.min(at, blocks - 1), 0)]
+                at = use * (rel - blocks) + (1 - use) * blocks
+                parts.append(own_split[lax.max(lax.min(at, blocks), 0)])
             else:
                 use = (1 - mine) * alive
-                at = use * (rel - blocks * after_own) + (1 - use) * (near_slot * blocks)
-                b = halo[lax.max(lax.min(at, 2 * blocks - 1), 0)]
-            parts.append(b * use.astype(F32))
-        return split2(jnp.concatenate(parts, axis=0))
-
-    def times(hi, lo, b_hi, b_lo):
-        both = jnp.dot(hi, jnp.concatenate([b_hi, b_lo], axis=1), preferred_element_type=F32)
-        return both[:, :width] + both[:, width:] + jnp.dot(lo, b_hi, preferred_element_type=F32)
+                at = use * (rel - blocks * after_own) + (1 - use) * (2 * blocks)
+                parts.append(halo_split[lax.max(lax.min(at, 2 * blocks), 0)])
+        return jnp.concatenate(parts, axis=0)
+
+    def times(a, b):
+        p = jnp.dot(a, b, preferred_element_type=F32)
+        return (p[:tile, :width] + p[tile:, width:]) + (p[:tile, width:] + p[tile:, :width])
 
     def at_block(row):
         return pl.ds(pl.multiple_of(row * tile, tile), tile)
@@ -150,20 +168,16 @@
         for j in range(group):
             row = i * group + j
             hi, lo = split2(jnp.concatenate([stage[k, j, s] for s in range(slots)], axis=1))
-            a_hi[row] = hi
-            a_lo[row] = lo
-            b_hi, b_lo = picked(row, True)
-            out[at_block(row), :] = times(hi, lo, b_hi, b_lo)
+            a = jnp.concatenate([hi, lo], axis=0)
+            a_split[row] = a
+            out[at_block(row), :] = times(a, picked(row, True))
 
     def halo_products(at_rows):
-        sums = []
-        for row in at_rows:
-            b_hi, b_lo = picked(row, False)
-            sums.append(out[at_block(row), :] + times(a_hi[row], a_lo[row], b_hi, b_lo))
+        sums = [out[at_block(row), :] + times(a_split[row], picked(row, False)) for row in at_rows]
         for row, total in zip(at_rows, sums):
             out[at_block(row), :] = total
 
-    @pl.loop(0, chunks + lag)
+    @pl.loop(0, chunks + 2 * lag)
     def _(i):
         @pl.when(i < chunks)
         def _():
@@ -180,44 +194,37 @@
             def _():
                 near(i + ahead).start()
 
-        @pl.when((i >= lag) & has_far)
+            split_halo(near_slot, i, c)
+
+        @pl.when((i >= lag) & (i < chunks + lag) & has_far)
         def _():
             far(i - lag).wait_recv()
             for d in range(1, n_cols):
                 sib(i - lag, 1, d).start()
-
-        @pl.when(i == 0)
-        def _():
-            bring_own.wait()
+            split_halo(far_slot, i - lag, c)
+
+        @pl.when((i >= lag) & (i < chunks + lag))
+        def _():
+            for d in range(1, n_cols):
+                sib(i - lag, 0, d, True).wait_recv()
+                split_halo(near_slot, i - lag, lax.rem(c + n_cols - d, n_cols))
+
+        @pl.when((i >= 2 * lag) & has_far)
+        def _():
+            for d in range(1, n_cols):
+                sib(i - 2 * lag, 1, d, True).wait_recv()
+                split_halo(far_slot, i - 2 * lag, lax.rem(c + n_cols - d, n_cols))
 
         @pl.when(i < chunks)
         def _():
             own_products(i)
-
-    @pl.loop(0, chunks)
-    def _(i):
-        for d in range(1, n_cols):
-            sib(i, 0, d, True).wait_recv()
-            sib(i, 0, d).wait_send()
-
-        @pl.when(has_far)
-        def _():
-            for d in range(1, n_cols):
-                sib(i, 1, d, True).wait_recv()
-                sib(i, 1, d).wait_send()
-
-        near(i).wait_send()
-
-        @pl.when(can_fwd)
-        def _():
-            far(i).wait_send()
 
     piece = part // pieces
     piece_blocks = piece // tile
     unroll = 2 if piece_blocks % 2 == 0 else 1
 
     def multiply_piece(col, i):
-        first = col * (part // tile) + i * piece_blocks
+        first = col * part_blocks + i * piece_blocks
 
         @pl.loop(0, piece_blocks // unroll)
         def _(j):
@@ -240,7 +247,7 @@
             multiply_piece(lax.rem(c + d, n_cols), i)
             give(i, d).start()
 
-    acc[0] = jnp.zeros_like(acc.at[0])
+    gram[...] = jnp.zeros_like(gram)
 
     @pl.loop(0, pieces)
     def _(i):
@@ -252,27 +259,73 @@
         out[piece_span(c, i), :] = x
         keep(i).start()
         hi, lo = split2(x)
-        both = jnp.concatenate([hi, lo], axis=1)
-        g = lax.dot_general(both, both, (((0,), (0,)), ((), ())), preferred_element_type=F32)
-        acc[0] += (g[:width, :width] + g[width:, width:]) + (g[:width, width:] + g[width:, :width])
+        gram[...] += lax.dot_general(hi, jnp.concatenate([hi, lo], axis=1), (((0,), (0,)), ((), ())),
+                                     preferred_element_type=F32)
+
+    cross = gram[:, width:]
+    gram[:, :width] = gram[:, :width] + (cross + cross.T)
+
+    half = width // n_cols
+
+    def half_span(col):
+        return pl.ds(pl.multiple_of(col * half, half), half)
+
+    def give_half(d):
+        return remote(gram.at[half_span(lax.rem(c + d, n_cols)), pl.ds(0, width)], halves.at[d - 1],
+                      half_s.at[d - 1], half_r.at[d - 1], siblings[d - 1])
+
+    for d in range(1, n_cols):
+        give_half(d).start()
+    total = gram[half_span(c), pl.ds(0, width)]
+    for d in range(1, n_cols):
+        give_half(d).wait_recv()
+        total = total + halves[d - 1]
+    acc[0] = total
 
     def add_up(s):
         return remote(acc.at[s], into.at[s], sum_s.at[s], sum_r.at[s], sum_peers[s])
 
-    for s in range(len(sum_peers)):
+    n_sums = len(sum_peers)
+    for s in range(n_sums):
         add_up(s).start()
         add_up(s).wait_recv()
         acc[s + 1] = acc[s] + into[s]
-    gram_out[...] = acc[len(sum_peers)]
-
-    for s in range(len(sum_peers)):
+
+    def hand_out(d):
+        return remote(acc.at[n_sums], full.at[half_span(c)], full_s.at[d - 1], full_r.at[d - 1], siblings[d - 1])
+
+    def hand_in(d):
+        return remote(acc.at[n_sums], full.at[half_span(lax.rem(c + n_cols - d, n_cols))],
+                      full_s.at[d - 1], full_r.at[d - 1], siblings[d - 1])
+
+    for d in range(1, n_cols):
+        hand_out(d).start()
+
+    all_sent(near_s, (partner, c))
+
+    @pl.when(can_fwd)
+    def _():
+        all_sent(far_s, (fwd_to, c))
+
+    for d in range(1, n_cols):
+        all_sent(sib_s.at[d - 1], siblings[d - 1])
+
+        @pl.when(has_far)
+        def _(d=d):
+            all_sent(sib_s.at[n_cols - 1 + d - 1], siblings[d - 1])
+
+        give_half(d).wait_send()
+        for i in range(pieces):
+            give(i, d).wait_send()
+    for s in range(n_sums):
         add_up(s).wait_send()
-
-    @pl.loop(0, pieces)
-    def _(i):
+    for i in range(pieces):
         keep(i).wait()
-        for d in range(1, n_cols):
-            give(i, d).wait_send()
+    full[half_span(c), :] = acc[n_sums]
+    for d in range(1, n_cols):
+        hand_in(d).wait_recv()
+        hand_out(d).wait_send()
+    gram_out[...] = full[...]
 
 
 def rows_and_gram(tile_cols, live_counts, block_vector, op_tiles, n_rows, n_cols):
@@ -283,9 +336,8 @@
     while part // chunks > tile:
         chunks *= 2
     pieces = 4
-    sums = int(math.log2(n_rows * n_cols))
-    n_sib = max(1, 2 * (n_cols - 1) * chunks)
-    n_give = max(1, (n_cols - 1) * pieces)
+    sums = int(math.log2(n_rows))
+    others = max(1, n_cols - 1)
     dma = pltpu.SemaphoreType.DMA
     vmem = pl.BlockSpec(memory_space=pltpu.VMEM)
     smem = pl.BlockSpec(memory_space=pltpu.SMEM)
@@ -297,21 +349,26 @@
         out_specs=(hbm, vmem),
         scratch_shapes=[
             pltpu.VMEM((blocks, tile, width), F32),
+            pltpu.VMEM((blocks + 1, tile, 2 * width), BF16),
             pltpu.VMEM((2 * blocks, tile, width), F32),
+            pltpu.VMEM((2 * blocks + 1, tile, 2 * width), BF16),
             pltpu.VMEM((2, blocks // chunks, slots, tile, tile), F32),
-            pltpu.VMEM((blocks, tile, slots * tile), BF16),
-            pltpu.VMEM((blocks, tile, slots * tile), BF16),
+            pltpu.VMEM((blocks, 2 * tile, slots * tile), BF16),
             pltpu.VMEM((rows, width), F32),
-            pltpu.VMEM((max(1, n_cols - 1), part, width), F32),
-            pltpu.VMEM((sums + 1, width, width), F32),
-            pltpu.VMEM((sums, width, width), F32),
+            pltpu.VMEM((others, part, width), F32),
+            pltpu.VMEM((width, 2 * width), F32),
+            pltpu.VMEM((others, width // n_cols, width), F32),
+            pltpu.VMEM((sums + 1, width // n_cols, width), F32),
+            pltpu.VMEM((sums, width // n_cols, width), F32),
+            pltpu.VMEM((width, width), F32),
             dma, dma((2,)), dma((pieces,)),
-            dma((chunks,)), dma((chunks,)), dma((chunks,)), dma((chunks,)), dma((n_sib,)), dma((n_sib,)),
-            dma((n_give,)), dma((n_give,)), dma((sums,)), dma((sums,)),
+            dma, dma((chunks,)), dma, dma((chunks,)), dma((2 * others,)), dma((2 * others * chunks,)),
+            dma((others * pieces,)), dma((others * pieces,)),
+            dma((others,)), dma((others,)), dma((sums,)), dma((sums,)), dma((others,)), dma((others,)),
         ],
-        compiler_params=pltpu.CompilerParams(collective_id=0, has_side_effects=True, vmem_limit_bytes=48 * MIB),
+        compiler_params=pltpu.CompilerParams(collective_id=0, has_side_effects=True, vmem_limit_bytes=56 * MIB),
         name="rows_and_gram",
-    )(tile_cols, live_counts, block_vector.reshape(blocks, tile, width), op_tiles)
+    )(tile_cols.T, live_counts, block_vector.reshape(blocks, tile, width), op_tiles)
 
 
 def spread(x):

time: 94.9 us -> 95.3 us (level)
  Pallas kernels: 92.6 us -> 91.4 us
  local copies, waits for them, and re-layouts: 1.43 us -> 2.42 us
    pallas_call x1, Pallas kernels: 86.2 us -> 85.1 us  [rows_and_gram(): pl.pallas_call(functools.partial(step_kernel, n_rows, n_cols, chunks, 8,...]
    unnamed x3 -> x4, local copies, waits for them, and re-layouts: 1.43 us -> 2.42 us
where the time goes in v3:
time: 95.3 us; the launch traced here: 94.5 us
  Pallas kernels  91.4 us (96%)
  local copies, waits for them, and re-layouts  2.42 us (3%)
    pallas_call x1, Pallas kernels, rows_and_gram(): pl.pallas_call(functools.partial(step_kernel, n_rows, n_cols, chunks, 8,...  85.1 us
    pallas_call x1, Pallas kernels, basis_of(): pl.pallas_call(functools.partial(basis_kernel, root), out_shape=(jax.Shap...  6.33 us
    unnamed x4, local copies, waits for them, and re-layouts  2.42 us

profile of v3, /device:TPU:2, one launch (start us, length us, event | category | flops | bytes accessed | tf_op | source)
XLA Modules:
  0.0 94.5 jit_solution(12202735593834606566)
XLA Ops:
  0.6 85.1 %rows_and_gram.1 = (f32[4096,128]{1,0:T(8,128)}, f32[128,128]{1,0:T(8,128)}) custom-call(s32[4,64]{1,0:T(4,128)} %bitcast.3, s32[64]{0:T(128)} %counts.1, f32[64,128,128]{2,1,0:T(8,128)} %bitcast.2, f32[64,4,128,128]{3,2,1,0:T(8,128)} %tiles.1), custom_call_target="tpu_custom_call" | custom-call | tf_op jit(solution)/shard_map/rows_and_gram/pallas_call | solution.py:345
  85.7 0.0 copy-start
  85.7 1.6 %copy-done = f32[4096,128]{1,0:T(8,128)S(1)} copy-done((f32[4096,128]{1,0:T(8,128)S(1)}, f32[4096,128]{1,0:T(8,128)}, u32[]{:S(2)}) %copy-start) | copy-done | bytes 2097176
  87.3 0.0 copy-start.1
  87.3 0.8 copy-done.1
  88.2 6.3 %factor_and_basis.1 = (f32[4096,128]{1,0:T(8,128)}, f32[128,128]{1,0:T(8,128)}) custom-call(f32[128,128]{1,0:T(8,128)S(1)} %copy-done.1, f32[4096,128]{1,0:T(8,128)S(1)} %copy-done), custom_call_target="tpu_custom_call" | custom-call | tf_op jit(solution)/shard_map/factor_and_basis/pallas_call | solution.py:437
Async XLA Ops:
  85.7 1.6 %copy-start = (f32[4096,128]{1,0:T(8,128)S(1)}, f32[4096,128]{1,0:T(8,128)}, u32[]{:S(2)}) copy-start(f32[4096,128]{1,0:T(8,128)} %get-tuple-element.5.rows) | copy-start | bytes 6291460
  87.3 0.8 copy-start.1

commit v4 on v3

--- a/solution.py
+++ b/solution.py
@@ -37,7 +37,7 @@
 
 
 def step_kernel(n_rows, n_cols, chunks, ahead, lag, pieces, cols, counts, own, tiles, rows_out, gram_out,
-                own_v, own_split, halo, halo_split, stage, a_split, out, got, gram, halves, acc, into, full,
+                own_split, halo, halo_split, stage, a_split, out, got, gram, halves, acc, into, full,
                 own_sem, stage_sem, rows_sem, near_s, near_r, far_s, far_r, sib_s, sib_r, part_s, part_r,
                 half_s, half_r, sum_s, sum_r, full_s, full_r):
     r = lax.axis_index("rows")
@@ -107,7 +107,7 @@
         k = lax.rem(i, 2)
         return pltpu.make_async_copy(tiles.at[pl.ds(i * group, group)], stage.at[k], stage_sem.at[k])
 
-    bring_own = pltpu.make_async_copy(own, own_v, own_sem)
+    bring_own = pltpu.make_async_copy(own, out, own_sem)
     bring_own.start()
     fetch(0).start()
     greet(peers)
@@ -125,7 +125,7 @@
 
     @pl.loop(0, blocks)
     def _(i):
-        hi, lo = split2(own_v[i])
+        hi, lo = split2(out[i])
         own_split[i] = jnp.concatenate([hi, lo], axis=1)
 
     before = (r - 1) * blocks
@@ -154,9 +154,6 @@
         p = jnp.dot(a, b, preferred_element_type=F32)
         return (p[:tile, :width] + p[tile:, width:]) + (p[:tile, width:] + p[tile:, :width])
 
-    def at_block(row):
-        return pl.ds(pl.multiple_of(row * tile, tile), tile)
-
     def own_products(i):
         k = lax.rem(i, 2)
         fetch(i).wait()
@@ -170,12 +167,7 @@
             hi, lo = split2(jnp.concatenate([stage[k, j, s] for s in range(slots)], axis=1))
             a = jnp.concatenate([hi, lo], axis=0)
             a_split[row] = a
-            out[at_block(row), :] = times(a, picked(row, True))
-
-    def halo_products(at_rows):
-        sums = [out[at_block(row), :] + times(a_split[row], picked(row, False)) for row in at_rows]
-        for row, total in zip(at_rows, sums):
-            out[at_block(row), :] = total
+            out[row] = times(a, picked(row, True))
 
     @pl.loop(0, chunks + 2 * lag)
     def _(i):
@@ -219,19 +211,20 @@
         def _():
             own_products(i)
 
-    piece = part // pieces
-    piece_blocks = piece // tile
-    unroll = 2 if piece_blocks % 2 == 0 else 1
+    piece_blocks = part_blocks // pieces
+    unroll = math.gcd(8, piece_blocks)
 
     def multiply_piece(col, i):
         first = col * part_blocks + i * piece_blocks
 
         @pl.loop(0, piece_blocks // unroll)
         def _(j):
-            halo_products([first + j * unroll + u for u in range(unroll)])
+            for u in range(unroll):
+                row = first + j * unroll + u
+                out[row] = out[row] + times(a_split[row], picked(row, False))
 
     def piece_span(col, i):
-        return pl.ds(pl.multiple_of(col * part + i * piece, piece), piece)
+        return pl.ds(col * part_blocks + i * piece_blocks, piece_blocks)
 
     def give(i, d):
         k = (d - 1) * pieces + i
@@ -252,13 +245,13 @@
     @pl.loop(0, pieces)
     def _(i):
         multiply_piece(c, i)
-        x = out[piece_span(c, i), :]
+        x = out[piece_span(c, i)]
         for d in range(1, n_cols):
             give(i, d).wait_recv()
-            x = x + got[d - 1, piece_span(0, i), :]
-        out[piece_span(c, i), :] = x
+            x = x + got[d - 1, piece_span(0, i)]
+        out[piece_span(c, i)] = x
         keep(i).start()
-        hi, lo = split2(x)
+        hi, lo = split2(x.reshape(piece_blocks * tile, width))
         gram[...] += lax.dot_general(hi, jnp.concatenate([hi, lo], axis=1), (((0,), (0,)), ((), ())),
                                      preferred_element_type=F32)
 
@@ -344,18 +337,20 @@
     hbm = pl.BlockSpec(memory_space=pl.ANY)
     return pl.pallas_call(
         functools.partial(step_kernel, n_rows, n_cols, chunks, 8, 2, pieces),
-        out_shape=(jax.ShapeDtypeStruct((part, width), F32), jax.ShapeDtypeStruct((width, width), F32)),
+        out_shape=(
+            jax.ShapeDtypeStruct((part // tile, tile, width), F32),
+            jax.ShapeDtypeStruct((width, width), F32),
+        ),
         in_specs=[smem, smem, hbm, hbm],
         out_specs=(hbm, vmem),
         scratch_shapes=[
-            pltpu.VMEM((blocks, tile, width), F32),
             pltpu.VMEM((blocks + 1, tile, 2 * width), BF16),
             pltpu.VMEM((2 * blocks, tile, width), F32),
             pltpu.VMEM((2 * blocks + 1, tile, 2 * width), BF16),
             pltpu.VMEM((2, blocks // chunks, slots, tile, tile), F32),
             pltpu.VMEM((blocks, 2 * tile, slots * tile), BF16),
-            pltpu.VMEM((rows, width), F32),
-            pltpu.VMEM((others, part, width), F32),
+            pltpu.VMEM((blocks, tile, width), F32),
+            pltpu.VMEM((others, part // tile, tile, width), F32),
             pltpu.VMEM((width, 2 * width), F32),
             pltpu.VMEM((others, width // n_cols, width), F32),
             pltpu.VMEM((sums + 1, width // n_cols, width), F32),
@@ -366,7 +361,7 @@
             dma((others * pieces,)), dma((others * pieces,)),
             dma((others,)), dma((others,)), dma((sums,)), dma((sums,)), dma((others,)), dma((others,)),
         ],
-        compiler_params=pltpu.CompilerParams(collective_id=0, has_side_effects=True, vmem_limit_bytes=56 * MIB),
+        compiler_params=pltpu.CompilerParams(collective_id=0, has_side_effects=True, vmem_limit_bytes=48 * MIB),
         name="rows_and_gram",
     )(tile_cols.T, live_counts, block_vector.reshape(blocks, tile, width), op_tiles)
 
@@ -455,7 +450,7 @@
 def on_device(n_rows, n_cols, block_vector, op_tiles, tile_cols, live_counts):
     rows, gram = rows_and_gram(tile_cols, live_counts, block_vector, op_tiles, n_rows, n_cols)
     root = math.sqrt(block_vector.shape[0] * n_rows)
-    return basis_of(gram, rows, root)
+    return basis_of(gram, rows.reshape(-1, rows.shape[2]), root)
 
 
 def solution(mesh):

time: 95.3 us -> 89.5 us (0.939)
  Pallas kernels: 91.4 us -> 86.8 us
  local copies, waits for them, and re-layouts: 2.42 us -> 1.33 us
    pallas_call x1, Pallas kernels: 85.1 us -> 80.4 us  [rows_and_gram(): pl.pallas_call(functools.partial(step_kernel, n_rows, n_cols, chunks, 8,...]
    unnamed x4, local copies, waits for them, and re-layouts: 2.42 us -> 1.33 us
where the time goes in v4:
time: 89.5 us; the launch traced here: 88.8 us
  Pallas kernels  86.8 us (97%)
  local copies, waits for them, and re-layouts  1.33 us (1%)
    pallas_call x1, Pallas kernels, rows_and_gram(): pl.pallas_call(functools.partial(step_kernel, n_rows, n_cols, chunks, 8,...  80.4 us
    pallas_call x1, Pallas kernels, basis_of(): pl.pallas_call(functools.partial(basis_kernel, root), out_shape=(jax.Shap...  6.37 us

profile of v4, /device:TPU:2, one launch (start us, length us, event | category | flops | bytes accessed | tf_op | source)
XLA Modules:
  0.0 88.8 jit_solution(6167369499369462680)
XLA Ops:
  0.6 0.0 copy-start
  0.6 0.7 copy-done
  1.3 0.0 copy-start.1
  1.3 0.7 copy-done.1
  2.0 80.4 %rows_and_gram.1 = (f32[32,128,128]{2,1,0:T(8,128)S(1)}, f32[128,128]{1,0:T(8,128)S(1)}) custom-call(s32[4,64]{1,0:T(4,128)S(1)} %bitcast.4, s32[64]{0:T(128)S(1)} %copy-done.1, f32[64,128,128]{2,1,0:T(8,128)} %bitcast.5, f32[64,4,128,128]{3,2,1,0:T(8,128)} %tiles.1), custom_call_target="tpu_custom_call" | custom-call | tf_op jit(solution)/shard_map/rows_and_gram/pallas_call | solution.py:338
  82.4 6.4 %factor_and_basis.1 = (f32[4096,128]{1,0:T(8,128)}, f32[128,128]{1,0:T(8,128)}) custom-call(f32[128,128]{1,0:T(8,128)S(1)} %get-tuple-element.4.gram, f32[4096,128]{1,0:T(8,128)S(1)} %bitcast.3), custom_call_target="tpu_custom_call" | custom-call | tf_op jit(solution)/shard_map/factor_and_basis/pallas_call | solution.py:432
Async XLA Ops:
  0.6 0.7 copy-start
  1.3 0.7 copy-start.1

commit v5 on v4

--- a/solution.py
+++ b/solution.py
@@ -36,9 +36,41 @@
     pl.semaphore_wait(barrier, total)
 
 
-def step_kernel(n_rows, n_cols, chunks, ahead, lag, pieces, cols, counts, own, tiles, rows_out, gram_out,
-                own_split, halo, halo_split, stage, a_split, out, got, gram, halves, acc, into, full,
-                own_sem, stage_sem, rows_sem, near_s, near_r, far_s, far_r, sib_s, sib_r, part_s, part_r,
+def rounds_of(n_rows):
+    rounds = []
+    stride = 1
+    while stride < n_rows:
+        radix = min(4, n_rows // stride)
+        rounds.append((stride, radix))
+        stride *= radix
+    return rounds
+
+
+def packed_rows(width, n_cols):
+    packed = width * 3 // 4
+    return packed if width == 128 and packed % (8 * n_cols) == 0 else width
+
+
+def pack(gram, rows):
+    n = gram.shape[0]
+    if rows == n:
+        return gram
+    h, q = n // 2, n // 4
+    lane = lax.broadcasted_iota(jnp.int32, (q, n), 1)
+    folded = jnp.where(lane < h, pltpu.roll(gram[h:h + q], h, axis=1), gram[h + q:])
+    return jnp.concatenate([gram[:h], folded], axis=0)
+
+
+def unpack(packed, n):
+    if packed.shape[0] == n:
+        return packed
+    folded = packed[n // 2:]
+    return jnp.concatenate([packed[:n // 2], pltpu.roll(folded, n // 2, axis=1), folded], axis=0)
+
+
+def step_kernel(n_rows, n_cols, chunks, ahead, lag, pieces, cols_in, counts_in, own, tiles, rows_out, gram_out,
+                cols, counts, own_split, halo, halo_split, stage, a_split, out, got, gram, sent, halves, acc, into, full,
+                small_sem, own_sem, stage_sem, rows_sem, near_s, near_r, far_s, far_r, sib_s, sib_r, part_s, part_r,
                 half_s, half_r, sum_s, sum_r, full_s, full_r):
     r = lax.axis_index("rows")
     c = lax.axis_index("cols")
@@ -56,14 +88,20 @@
     near_slot = 1 - odd
     far_slot = odd
     siblings = [(r, lax.rem(c + d, n_cols)) for d in range(1, n_cols)]
-    sum_peers = []
-    for b in range(int(math.log2(n_rows))):
-        bit = lax.rem(r // (1 << b), 2)
-        sum_peers.append((r + (1 << b) * (1 - 2 * bit), c))
+    sum_rounds = []
+    for first, radix in rounds_of(n_rows):
+        digit = lax.rem(r // first, radix)
+        low, high = lax.rem(digit, 2), digit // 2
+        others = []
+        for k in range(1, radix):
+            new_low = 1 - low if k % 2 else low
+            new_high = 1 - high if k // 2 else high
+            others.append((r + (new_low - low + 2 * (new_high - high)) * first, c))
+        sum_rounds.append(others)
 
     peers = [(None, (partner, c)), (can_fwd, (fwd_to, c)), (has_far, (far_from, c))]
     peers += [(None, device) for device in siblings]
-    peers += [(None, device) for device in sum_peers[1:]]
+    peers += [(None, device) for others in sum_rounds for device in others if device is not sum_rounds[0][0]]
 
     def remote(src, dst, send_sem, recv_sem, device):
         return pltpu.make_async_remote_copy(
@@ -107,6 +145,10 @@
         k = lax.rem(i, 2)
         return pltpu.make_async_copy(tiles.at[pl.ds(i * group, group)], stage.at[k], stage_sem.at[k])
 
+    bring_cols = pltpu.make_async_copy(cols_in, cols, small_sem.at[0])
+    bring_counts = pltpu.make_async_copy(counts_in, counts, small_sem.at[1])
+    bring_cols.start()
+    bring_counts.start()
     bring_own = pltpu.make_async_copy(own, out, own_sem)
     bring_own.start()
     fetch(0).start()
@@ -121,6 +163,8 @@
 
     own_split[blocks] = jnp.zeros((tile, 2 * width), BF16)
     halo_split[2 * blocks] = jnp.zeros((tile, 2 * width), BF16)
+    bring_cols.wait()
+    bring_counts.wait()
     bring_own.wait()
 
     @pl.loop(0, blocks)
@@ -256,33 +300,40 @@
                                      preferred_element_type=F32)
 
     cross = gram[:, width:]
-    gram[:, :width] = gram[:, :width] + (cross + cross.T)
-
-    half = width // n_cols
+    sent[...] = pack(gram[:, :width] + (cross + cross.T), sent.shape[0])
+
+    half = sent.shape[0] // n_cols
 
     def half_span(col):
         return pl.ds(pl.multiple_of(col * half, half), half)
 
     def give_half(d):
-        return remote(gram.at[half_span(lax.rem(c + d, n_cols)), pl.ds(0, width)], halves.at[d - 1],
+        return remote(sent.at[half_span(lax.rem(c + d, n_cols))], halves.at[d - 1],
                       half_s.at[d - 1], half_r.at[d - 1], siblings[d - 1])
 
     for d in range(1, n_cols):
         give_half(d).start()
-    total = gram[half_span(c), pl.ds(0, width)]
+    total = sent[half_span(c), :]
     for d in range(1, n_cols):
         give_half(d).wait_recv()
         total = total + halves[d - 1]
     acc[0] = total
 
-    def add_up(s):
-        return remote(acc.at[s], into.at[s], sum_s.at[s], sum_r.at[s], sum_peers[s])
-
-    n_sums = len(sum_peers)
+    def add_up(s, k):
+        at = 3 * s + k
+        return remote(acc.at[s], into.at[at], sum_s.at[at], sum_r.at[at], sum_rounds[s][k])
+
+    n_sums = len(sum_rounds)
     for s in range(n_sums):
-        add_up(s).start()
-        add_up(s).wait_recv()
-        acc[s + 1] = acc[s] + into[s]
+        n_others = len(sum_rounds[s])
+        for k in range(n_others):
+            add_up(s, k).start()
+        for k in range(n_others):
+            add_up(s, k).wait_recv()
+        total = acc[s] + into[3 * s]
+        if n_others == 3:
+            total = total + (into[3 * s + 1] + into[3 * s + 2])
+        acc[s + 1] = total
 
     def hand_out(d):
         return remote(acc.at[n_sums], full.at[half_span(c)], full_s.at[d - 1], full_r.at[d - 1], siblings[d - 1])
@@ -311,14 +362,15 @@
         for i in range(pieces):
             give(i, d).wait_send()
     for s in range(n_sums):
-        add_up(s).wait_send()
+        for k in range(len(sum_rounds[s])):
+            add_up(s, k).wait_send()
     for i in range(pieces):
         keep(i).wait()
     full[half_span(c), :] = acc[n_sums]
     for d in range(1, n_cols):
         hand_in(d).wait_recv()
         hand_out(d).wait_send()
-    gram_out[...] = full[...]
+    gram_out[...] = unpack(full[...], width)
 
 
 def rows_and_gram(tile_cols, live_counts, block_vector, op_tiles, n_rows, n_cols):
@@ -329,11 +381,13 @@
     while part // chunks > tile:
         chunks *= 2
     pieces = 4
-    sums = int(math.log2(n_rows))
+    sums = len(rounds_of(n_rows))
     others = max(1, n_cols - 1)
+    packed = packed_rows(width, n_cols)
+    half = packed // n_cols
     dma = pltpu.SemaphoreType.DMA
     vmem = pl.BlockSpec(memory_space=pltpu.VMEM)
-    smem = pl.BlockSpec(memory_space=pltpu.SMEM)
+    small = pl.BlockSpec(memory_space=pltpu.HBM)
     hbm = pl.BlockSpec(memory_space=pl.ANY)
     return pl.pallas_call(
         functools.partial(step_kernel, n_rows, n_cols, chunks, 8, 2, pieces),
@@ -341,9 +395,11 @@
             jax.ShapeDtypeStruct((part // tile, tile, width), F32),
             jax.ShapeDtypeStruct((width, width), F32),
         ),
-        in_specs=[smem, smem, hbm, hbm],
+        in_specs=[small, small, hbm, hbm],
         out_specs=(hbm, vmem),
         scratch_shapes=[
+            pltpu.SMEM((slots, blocks), jnp.int32),
+            pltpu.SMEM((blocks,), jnp.int32),
             pltpu.VMEM((blocks + 1, tile, 2 * width), BF16),
             pltpu.VMEM((2 * blocks, tile, width), F32),
             pltpu.VMEM((2 * blocks + 1, tile, 2 * width), BF16),
@@ -352,14 +408,15 @@
             pltpu.VMEM((blocks, tile, width), F32),
             pltpu.VMEM((others, part // tile, tile, width), F32),
             pltpu.VMEM((width, 2 * width), F32),
-            pltpu.VMEM((others, width // n_cols, width), F32),
-            pltpu.VMEM((sums + 1, width // n_cols, width), F32),
-            pltpu.VMEM((sums, width // n_cols, width), F32),
-            pltpu.VMEM((width, width), F32),
-            dma, dma((2,)), dma((pieces,)),
+            pltpu.VMEM((packed, width), F32),
+            pltpu.VMEM((others, half, width), F32),
+            pltpu.VMEM((sums + 1, half, width), F32),
+            pltpu.VMEM((3 * sums, half, width), F32),
+            pltpu.VMEM((packed, width), F32),
+            dma((2,)), dma, dma((2,)), dma((pieces,)),
             dma, dma((chunks,)), dma, dma((chunks,)), dma((2 * others,)), dma((2 * others * chunks,)),
             dma((others * pieces,)), dma((others * pieces,)),
-            dma((others,)), dma((others,)), dma((sums,)), dma((sums,)), dma((others,)), dma((others,)),
+            dma((others,)), dma((others,)), dma((3 * sums,)), dma((3 * sums,)), dma((others,)), dma((others,)),
         ],
         compiler_params=pltpu.CompilerParams(collective_id=0, has_side_effects=True, vmem_limit_bytes=48 * MIB),
         name="rows_and_gram",

time: 89.5 us -> 85.4 us (0.954)
  Pallas kernels: 86.8 us -> 82 us
    pallas_call x1, Pallas kernels: 80.4 us -> 75.6 us  [rows_and_gram(): pl.pallas_call(functools.partial(step_kernel, n_rows, n_cols, chunks, 8,...]
where the time goes in v5:
time: 85.4 us; the launch traced here: 83.9 us
  Pallas kernels  82 us (96%)
  local copies, waits for them, and re-layouts  1.33 us (2%)
    pallas_call x1, Pallas kernels, rows_and_gram(): pl.pallas_call(functools.partial(step_kernel, n_rows, n_cols, chunks, 8,...  75.6 us
    pallas_call x1, Pallas kernels, basis_of(): pl.pallas_call(functools.partial(basis_kernel, root), out_shape=(jax.Shap...  6.37 us

profile of v5, /device:TPU:2, one launch (start us, length us, event | category | flops | bytes accessed | tf_op | source)
XLA Modules:
  0.0 83.9 jit_solution(10351843116405948447)
XLA Ops:
  0.6 0.0 copy-start
  0.6 0.7 copy-done
  1.3 0.0 copy-start.1
  1.3 0.7 copy-done.1
  2.0 75.6 %rows_and_gram.1 = (f32[32,128,128]{2,1,0:T(8,128)S(1)}, f32[128,128]{1,0:T(8,128)S(1)}) custom-call(s32[4,64]{1,0:T(4,128)S(1)} %bitcast.4, s32[64]{0:T(128)S(1)} %copy-done.1, f32[64,128,128]{2,1,0:T(8,128)} %bitcast.5, f32[64,4,128,128]{3,2,1,0:T(8,128)} %tiles.1), custom_call_target="tpu_custom_call" | custom-call | tf_op jit(solution)/shard_map/rows_and_gram/pallas_call | solution.py:392
  77.6 6.4 %factor_and_basis.1 = (f32[4096,128]{1,0:T(8,128)}, f32[128,128]{1,0:T(8,128)}) custom-call(f32[128,128]{1,0:T(8,128)S(1)} %get-tuple-element.4.gram, f32[4096,128]{1,0:T(8,128)S(1)} %bitcast.3), custom_call_target="tpu_custom_call" | custom-call | tf_op jit(solution)/shard_map/factor_and_basis/pallas_call | solution.py:489
Async XLA Ops:
  0.6 0.7 copy-start
  1.3 0.7 copy-start.1

commit v6 on v5

--- a/solution.py
+++ b/solution.py
@@ -163,14 +163,15 @@
 
     own_split[blocks] = jnp.zeros((tile, 2 * width), BF16)
     halo_split[2 * blocks] = jnp.zeros((tile, 2 * width), BF16)
-    bring_cols.wait()
-    bring_counts.wait()
-    bring_own.wait()
-
-    @pl.loop(0, blocks)
-    def _(i):
-        hi, lo = split2(out[i])
-        own_split[i] = jnp.concatenate([hi, lo], axis=1)
+
+    split_steps = 2 * lag
+    per_step = blocks // split_steps
+
+    def split_own(i):
+        @pl.loop(0, per_step)
+        def _(j):
+            hi, lo = split2(out[i * per_step + j])
+            own_split[i * per_step + j] = jnp.concatenate([hi, lo], axis=1)
 
     before = (r - 1) * blocks
     first_slot = c * slots
@@ -251,9 +252,19 @@
                 sib(i - 2 * lag, 1, d, True).wait_recv()
                 split_halo(far_slot, i - 2 * lag, lax.rem(c + n_cols - d, n_cols))
 
-        @pl.when(i < chunks)
-        def _():
-            own_products(i)
+        @pl.when(i == 0)
+        def _():
+            bring_own.wait()
+            bring_cols.wait()
+            bring_counts.wait()
+
+        @pl.when(i < split_steps)
+        def _():
+            split_own(i)
+
+        @pl.when(i >= split_steps)
+        def _():
+            own_products(i - split_steps)
 
     piece_blocks = part_blocks // pieces
     unroll = math.gcd(8, piece_blocks)

time: 85.4 us -> 86.8 us (1.016)
  Pallas kernels: 82 us -> 83.1 us
    pallas_call x1, Pallas kernels: 75.6 us -> 76.7 us  [rows_and_gram(): pl.pallas_call(functools.partial(step_kernel, n_rows, n_cols, chunks, 8,...]
where the time goes in v6:
time: 86.8 us; the launch traced here: 85.1 us
  Pallas kernels  83.1 us (96%)
  local copies, waits for them, and re-layouts  1.33 us (2%)
    pallas_call x1, Pallas kernels, rows_and_gram(): pl.pallas_call(functools.partial(step_kernel, n_rows, n_cols, chunks, 8,...  76.7 us
    pallas_call x1, Pallas kernels, basis_of(): pl.pallas_call(functools.partial(basis_kernel, root), out_shape=(jax.Shap...  6.37 us

profile of v6, /device:TPU:2, one launch (start us, length us, event | category | flops | bytes accessed | tf_op | source)
XLA Modules:
  0.0 85.1 jit_solution(6835078006843294629)
XLA Ops:
  0.6 0.0 copy-start
  0.6 0.7 copy-done
  1.3 0.0 copy-start.1
  1.3 0.7 copy-done.1
  2.0 76.7 %rows_and_gram.1 = (f32[32,128,128]{2,1,0:T(8,128)S(1)}, f32[128,128]{1,0:T(8,128)S(1)}) custom-call(s32[4,64]{1,0:T(4,128)S(1)} %bitcast.4, s32[64]{0:T(128)S(1)} %copy-done.1, f32[64,128,128]{2,1,0:T(8,128)} %bitcast.5, f32[64,4,128,128]{3,2,1,0:T(8,128)} %tiles.1), custom_call_target="tpu_custom_call" | custom-call | tf_op jit(solution)/shard_map/rows_and_gram/pallas_call | solution.py:403
  78.7 6.4 %factor_and_basis.1 = (f32[4096,128]{1,0:T(8,128)}, f32[128,128]{1,0:T(8,128)}) custom-call(f32[128,128]{1,0:T(8,128)S(1)} %get-tuple-element.4.gram, f32[4096,128]{1,0:T(8,128)S(1)} %bitcast.3), custom_call_target="tpu_custom_call" | custom-call | tf_op jit(solution)/shard_map/factor_and_basis/pallas_call | solution.py:500
Async XLA Ops:
  0.6 0.7 copy-start
  1.3 0.7 copy-start.1

commit v7 on v5

--- a/solution.py
+++ b/solution.py
@@ -139,7 +139,8 @@
         whole = halo.at[pl.ds(near_slot * blocks + c * part_blocks, part_blocks)]
         remote(whole, whole, sem, near_r.at[0], device).wait_send()
 
-    group = blocks // chunks
+    group = 2 * (blocks // chunks)
+    fetches = chunks // 2
 
     def fetch(i):
         k = lax.rem(i, 2)
@@ -202,7 +203,7 @@
         k = lax.rem(i, 2)
         fetch(i).wait()
 
-        @pl.when(i + 1 < chunks)
+        @pl.when(i + 1 < fetches)
         def _():
             fetch(i + 1).start()
 
@@ -251,9 +252,9 @@
                 sib(i - 2 * lag, 1, d, True).wait_recv()
                 split_halo(far_slot, i - 2 * lag, lax.rem(c + n_cols - d, n_cols))
 
-        @pl.when(i < chunks)
+        @pl.when((i < chunks) & (lax.rem(i, 2) == 0))
         def _():
-            own_products(i)
+            own_products(i // 2)
 
     piece_blocks = part_blocks // pieces
     unroll = math.gcd(8, piece_blocks)
@@ -403,7 +404,7 @@
             pltpu.VMEM((blocks + 1, tile, 2 * width), BF16),
             pltpu.VMEM((2 * blocks, tile, width), F32),
             pltpu.VMEM((2 * blocks + 1, tile, 2 * width), BF16),
-            pltpu.VMEM((2, blocks // chunks, slots, tile, tile), F32),
+            pltpu.VMEM((2, 2 * (blocks // chunks), slots, tile, tile), F32),
             pltpu.VMEM((blocks, 2 * tile, slots * tile), BF16),
             pltpu.VMEM((blocks, tile, width), F32),
             pltpu.VMEM((others, part // tile, tile, width), F32),

time: 85.4 us -> 86 us (level)
  no operation moved by 1% of the time
where the time goes in v7:
time: 86 us; the launch traced here: 84.6 us
  Pallas kernels  82.6 us (96%)
  local copies, waits for them, and re-layouts  1.33 us (2%)
    pallas_call x1, Pallas kernels, rows_and_gram(): pl.pallas_call(functools.partial(step_kernel, n_rows, n_cols, chunks, 8,...  76.3 us
    pallas_call x1, Pallas kernels, basis_of(): pl.pallas_call(functools.partial(basis_kernel, root), out_shape=(jax.Shap...  6.36 us

profile of v7, /device:TPU:2, one launch (start us, length us, event | category | flops | bytes accessed | tf_op | source)
XLA Modules:
  0.0 84.6 jit_solution(8942937222894503118)
XLA Ops:
  0.6 0.0 copy-start
  0.6 0.7 copy-done
  1.3 0.0 copy-start.1
  1.3 0.7 copy-done.1
  2.0 76.3 %rows_and_gram.1 = (f32[32,128,128]{2,1,0:T(8,128)S(1)}, f32[128,128]{1,0:T(8,128)S(1)}) custom-call(s32[4,64]{1,0:T(4,128)S(1)} %bitcast.4, s32[64]{0:T(128)S(1)} %copy-done.1, f32[64,128,128]{2,1,0:T(8,128)} %bitcast.5, f32[64,4,128,128]{3,2,1,0:T(8,128)} %tiles.1), custom_call_target="tpu_custom_call" | custom-call | tf_op jit(solution)/shard_map/rows_and_gram/pallas_call | solution.py:393
  78.3 6.4 %factor_and_basis.1 = (f32[4096,128]{1,0:T(8,128)}, f32[128,128]{1,0:T(8,128)}) custom-call(f32[128,128]{1,0:T(8,128)S(1)} %get-tuple-element.4.gram, f32[4096,128]{1,0:T(8,128)S(1)} %bitcast.3), custom_call_target="tpu_custom_call" | custom-call | tf_op jit(solution)/shard_map/factor_and_basis/pallas_call | solution.py:490
Async XLA Ops:
  0.6 0.7 copy-start
  1.3 0.7 copy-start.1
